TPU v7x, 32 devices: a whole 2x2x4 slice. The times are simulated.
32 devices in a mesh: dp: 2 (over core), hid: 4 (over y, x), mod: 4 (over z).
Axes of the slice: x: 2, y: 2, z: 4, core: 2. Of those that a mesh axis runs over, the one named last changes fastest.
Arguments:
- patches: bfloat16 [4, 1625088], P('mod', ('dp', 'hid')), may hold values from -6 to 6
- visible: int32 [16], P(('dp', 'hid')), may hold values from 265 to 529, as said below
- project_in: bfloat16 [3, 768, 768], P(None, ('dp', 'hid'), 'mod'), may hold values from -0.21875 to 0.21875
- project_out: bfloat16 [768, 768], P('mod', ('dp', 'hid')), may hold values from -1.5 to 1.5
- expand: bfloat16 [768, 3072], P('mod', ('dp', 'hid')), may hold values from -0.21875 to 0.21875
- contract: bfloat16 [3072, 768], P(('dp', 'hid'), 'mod'), may hold values from -0.109375 to 0.109375
- expand_bias: bfloat16 [3072], P(('dp', 'hid')), may hold values from -1.5 to 1.5
- vectors: float32 [8, 768], P(None, 'mod'), may hold values from -1.2 to 1.8, as said below
- cotangent: bfloat16 [4, 1625088], P('mod', ('dp', 'hid')), may hold values from -6 to 6
Outputs:
- output: bfloat16 [4, 1625088], P('mod', ('dp', 'hid'))
- input_grad: float32 [4, 1625088], P('mod', ('dp', 'hid'))
- project_in_grad: float32 [3, 768, 768], P(None, ('dp', 'hid'), 'mod')
- project_out_grad: float32 [768, 768], P('mod', ('dp', 'hid'))
- expand_grad: float32 [768, 3072], P('mod', ('dp', 'hid'))
- contract_grad: float32 [3072, 768], P(('dp', 'hid'), 'mod')
- expand_bias_grad: float32 [3072], P(('dp', 'hid'))
- vectors_grad: float32 [8, 768], P(None, 'mod')
Inputs may be any that keep to these rules, and one draw needn't show every extreme that they name: visible patches of each strip; in every draw some strip keeps all 529. `vectors`: rows 0 and 5 are gains, the other rows biases.
All inputs are finite; a program needn't handle non-finite values.
Results may differ from a plain program's by a relative error of at most 0.019.
Values may be sent and summed in bfloat16 or wider, within the bound.
No kernel may reach another device: no remote copies, remote signals or barrier semaphores. Data moves between devices by JAX's collectives and lax.ppermute only.
A program may use at most 128 MiB of HBM per device.

v0:
```python
from functools import partial

import jax
import jax.numpy as jnp
from jax import lax
from jax.sharding import PartitionSpec as P

D = 768
HEAD_DIM = 64
L = 529


eps = 1e-06
bf16 = jnp.bfloat16
f32 = jnp.float32


def split_up(shard, dim, count):
    lengths = shard.shape
    tiles = shard.reshape(*lengths[:dim], count, lengths[dim] // count, *lengths[dim + 1 :])
    return jnp.moveaxis(tiles, dim, 0)


def sent_and_summed(shard, axis, dim):
    count = lax.axis_size(axis)
    tiles = lax.all_to_all(split_up(shard, dim, count), axis, 0, 0, tiled=True)
    return jnp.sum(tiles.astype(jnp.float32), axis=0)


def feature_sums(first, second):
    return lax.psum((first, second), "mod")


def features(values):
    return lax.all_gather(values, "mod", axis=1, tiled=True)


def heads_sum(values):
    return lax.psum_scatter(
        values.astype(jnp.bfloat16), "mod", scatter_dimension=1, tiled=True
    ).astype(jnp.float32)


def group_rows(values):
    return lax.all_gather(values, "hid", axis=0, tiled=True)


def group_sums(values):
    return lax.psum_scatter(
        values.astype(jnp.bfloat16), "hid", scatter_dimension=0, tiled=True
    ).astype(jnp.float32)


def hidden_rows(values):
    return lax.all_gather(values, "mod", axis=0, tiled=True)


def row_exchange(values):
    return lax.all_to_all(values, "mod", split_axis=0, concat_axis=1, tiled=True)


def norm_forward(values, gain, shift):
    total, squares = feature_sums(jnp.sum(values, 1), jnp.sum(values * values, 1))
    center = total / D
    inverse = lax.rsqrt(squares / D - center * center + eps)
    normed = (values - center[:, None]) * inverse[:, None]
    return (normed, inverse, normed * gain + shift)


def norm_backward(grad_in, normed, inverse, gain):
    scaled = grad_in * gain
    total, cross = feature_sums(jnp.sum(scaled, 1), jnp.sum(scaled * normed, 1))
    result = inverse[:, None] * (scaled - total[:, None] / D - normed * cross[:, None] / D)
    return (result, jnp.sum(grad_in * normed, 0), jnp.sum(grad_in, 0))


def masked_logits(queries, keys, count):
    logits = jnp.einsum("qhc,khc->hqk", queries, keys, preferred_element_type=f32) * HEAD_DIM ** (
        -0.5
    )
    keep = (jnp.arange(queries.shape[0]) < count)[None, None, :]
    return jnp.where(keep, logits, -1e30)


def attend_forward(item):
    queries, keys, values, count = item
    logits = masked_logits(queries, keys, count)
    top = jnp.max(logits, -1, keepdims=True)
    expo = jnp.exp(logits - top)
    total = jnp.sum(expo, -1, keepdims=True)
    chance = (expo / total).astype(bf16)
    mixed = jnp.einsum("hqk,khc->qhc", chance, values, preferred_element_type=f32)
    return (mixed, (top + jnp.log(total))[..., 0])


def attend_backward(item):
    queries, keys, values, count, log_total, grad_mixed = item
    logits = masked_logits(queries, keys, count)
    chance = jnp.exp(logits - log_total[..., None])
    grad_chance = jnp.einsum("qhc,khc->hqk", grad_mixed, values, preferred_element_type=f32)
    grad_values = jnp.einsum(
        "hqk,qhc->khc", chance.astype(bf16), grad_mixed, preferred_element_type=f32
    )
    inner = jnp.sum(chance * grad_chance, -1, keepdims=True)
    grad_logits = (chance * (grad_chance - inner)).astype(bf16)
    grad_queries = jnp.einsum(
        "hqk,khc->qhc", grad_logits, keys, preferred_element_type=f32
    ) * HEAD_DIM ** (-0.5)
    grad_keys = jnp.einsum(
        "hqk,qhc->khc", grad_logits, queries, preferred_element_type=f32
    ) * HEAD_DIM ** (-0.5)
    return (grad_queries.astype(bf16), grad_keys.astype(bf16), grad_values.astype(bf16))


def body(
    patches, visible, project_in, project_out, expand, contract, expand_bias, vectors, cotangent
):
    strips = visible.shape[0]
    length = L
    part = D // lax.axis_size("mod")
    rows = strips * length
    heads_here = part // HEAD_DIM
    stream = patches.astype(f32).reshape(rows, part)
    valid = (jnp.arange(length)[None, :] < visible[:, None]).astype(f32).reshape(rows, 1)
    in_full, out_full = (
        lax.all_gather(project_in, ("dp", "hid"), axis=1, tiled=True),
        lax.all_gather(project_out, ("dp", "hid"), axis=1, tiled=True),
    )
    w_in, w_out, bias_in = (
        lax.all_gather(expand, "dp", axis=1, tiled=True),
        lax.all_gather(contract, "dp", axis=0, tiled=True),
        lax.all_gather(expand_bias, "dp", axis=0, tiled=True),
    )
    normed_attn, inverse_attn, shifted_attn = norm_forward(stream, vectors[0], vectors[1])
    attn_inputs = features(shifted_attn.astype(bf16))
    projected = jnp.einsum("rd,tdc->trc", attn_inputs, in_full, preferred_element_type=f32)
    shape_heads = (strips, length, heads_here, HEAD_DIM)
    queries = (projected[0] + vectors[2]).astype(bf16).reshape(shape_heads)
    keys = projected[1].astype(bf16).reshape(shape_heads)
    values = (projected[2] + vectors[3]).astype(bf16).reshape(shape_heads)
    mixed, log_total = lax.map(attend_forward, (queries, keys, values, visible))
    mixed_low = mixed.reshape(rows, part).astype(bf16)
    branch = heads_sum(jnp.dot(mixed_low, out_full, preferred_element_type=f32)) + vectors[4]
    resid = stream + branch
    normed_mlp, inverse_mlp, shifted_mlp = norm_forward(resid, vectors[5], vectors[6])
    group_in = group_rows(shifted_mlp.astype(bf16))
    wide_in, wide_out = (
        lax.all_gather(w_in, "mod", axis=0, tiled=True),
        lax.all_gather(w_out, "mod", axis=1, tiled=True),
    )
    spread_in = row_exchange(group_in)
    pre = jnp.dot(spread_in, wide_in, preferred_element_type=f32) + bias_in
    hidden = jax.nn.gelu(pre, approximate=False).astype(bf16)
    hidden_all = hidden_rows(hidden)
    mlp_out = group_sums(jnp.dot(hidden_all, w_out, preferred_element_type=f32)) + vectors[7]
    result = (valid * (resid + mlp_out)).astype(bf16).reshape(1, rows * part)
    grad_out = cotangent.astype(f32).reshape(rows, part) * valid
    grad_mlp = grad_out.astype(bf16)
    group_grad = group_rows(grad_mlp)
    grad_contract = jnp.einsum("rf,rd->fd", hidden_all, group_grad, preferred_element_type=f32)
    spread_grad = row_exchange(group_grad)
    grad_hidden = jnp.einsum("rd,fd->rf", spread_grad, wide_out, preferred_element_type=f32)
    slope = jax.vjp(partial(jax.nn.gelu, approximate=False), pre)[1](grad_hidden)[0]
    grad_pre = slope.astype(bf16)
    group_pre = hidden_rows(grad_pre)
    grad_expand = jnp.einsum("rd,rf->df", group_in, group_pre, preferred_element_type=f32)
    grad_bias_in = jnp.sum(group_pre.astype(f32), 0)
    grad_normed_mlp = group_sums(
        jnp.einsum("rf,df->rd", group_pre, w_in, preferred_element_type=f32)
    )
    back_mlp, gain_mlp, shift_mlp = norm_backward(
        grad_normed_mlp, normed_mlp, inverse_mlp, vectors[5]
    )
    grad_resid = grad_out + back_mlp
    grad_branch = grad_resid.astype(bf16)
    branch_all = features(grad_branch)
    grad_project_out = jnp.einsum("re,rd->ed", mixed_low, branch_all, preferred_element_type=f32)
    grad_mixed = jnp.einsum("rd,ed->re", branch_all, out_full, preferred_element_type=f32).astype(
        bf16
    )
    grad_queries, grad_keys, grad_values = lax.map(
        attend_backward,
        (queries, keys, values, visible, log_total, grad_mixed.reshape(shape_heads)),
    )
    stacked = jnp.stack(
        [
            grad_queries.reshape(rows, part),
            grad_keys.reshape(rows, part),
            grad_values.reshape(rows, part),
        ]
    )
    grad_project_in = jnp.einsum("rd,trc->tdc", attn_inputs, stacked, preferred_element_type=f32)
    grad_normed_attn = heads_sum(
        jnp.einsum("trc,tdc->rd", stacked, in_full, preferred_element_type=f32)
    )
    back_attn, gain_attn, shift_attn = norm_backward(
        grad_normed_attn, normed_attn, inverse_attn, vectors[0]
    )
    grad_input = (grad_resid + back_attn).reshape(1, rows * part)
    vector_parts = jnp.stack(
        [
            gain_attn,
            shift_attn,
            jnp.sum(stacked[0].astype(f32), 0),
            jnp.sum(stacked[2].astype(f32), 0),
            jnp.sum(grad_branch.astype(f32), 0),
            gain_mlp,
            shift_mlp,
            jnp.sum(grad_mlp.astype(f32), 0),
        ]
    )
    vector_grad = lax.psum(vector_parts, ("dp", "hid"))
    in_grad, out_grad = (
        sent_and_summed(grad_project_in.astype(jnp.bfloat16), ("dp", "hid"), 1),
        sent_and_summed(grad_project_out.astype(jnp.bfloat16), ("dp", "hid"), 1),
    )
    expand_grad, contract_grad, bias_grad = (
        lax.psum_scatter(
            grad_expand.astype(jnp.bfloat16), "dp", scatter_dimension=1, tiled=True
        ).astype(jnp.float32),
        lax.psum_scatter(
            grad_contract.astype(jnp.bfloat16), "dp", scatter_dimension=0, tiled=True
        ).astype(jnp.float32),
        lax.psum_scatter(
            grad_bias_in.astype(jnp.bfloat16), "dp", scatter_dimension=0, tiled=True
        ).astype(jnp.float32),
    )
    return (
        result,
        grad_input,
        in_grad,
        out_grad,
        expand_grad,
        contract_grad,
        bias_grad,
        vector_grad,
    )


def solution(mesh):
    in_specs = (
        P("mod", ("dp", "hid")),
        P(("dp", "hid")),
        P(None, ("dp", "hid"), "mod"),
        P("mod", ("dp", "hid")),
        P("mod", ("dp", "hid")),
        P(("dp", "hid"), "mod"),
        P(("dp", "hid")),
        P(None, "mod"),
        P("mod", ("dp", "hid")),
    )
    out_specs = (
        P("mod", ("dp", "hid")),
        P("mod", ("dp", "hid")),
        P(None, ("dp", "hid"), "mod"),
        P("mod", ("dp", "hid")),
        P("mod", ("dp", "hid")),
        P(("dp", "hid"), "mod"),
        P(("dp", "hid")),
        P(None, "mod"),
    )
    return jax.shard_map(body, mesh=mesh, in_specs=in_specs, out_specs=out_specs, check_vma=False)
```

profile of v0, /device:TPU:0, one launch (start us, length us, event | category | flops | bytes accessed | tf_op | source)
XLA Modules:
  0.0 881.0 jit_solution(17102044931781089497)
XLA Ops:
  7.2 8.6 convert_reduce_fusion.8
  17.5 20.5 %all-reduce.6 = (f32[1058]{0:T(1024)S(1)}, f32[1058]{0:T(1024)S(1)}) all-reduce(f32[1058]{0:T(1024)S(1)} %get-tuple-element.171, f32[1058]{0:T(1024)S(1)} %get-tuple-element.170), channel_id=1, replica_groups=mesh['dp'=2,'hid'=4,'mod'=4] {'mod'}, use_global_device_ids=true, to_apply=%region_3.0 | all-reduce | flops 2116 | bytes 16928 | tf_op jit(solution)/shard_map/psum | solution.py:31
  39.5 33.3 %all_gather.40 = bf16[3,768,192]{2,0,1:T(4,128)(2,1)S(1)} all-gather(bf16[3,96,192]{2,0,1:T(4,128)(2,1)S(1)} %copy.58), channel_id=1, replica_groups=mesh['dp'=2,'hid'=4,'mod'=4] {'dp','hid'}, dimensions={1}, use_global_device_ids=true | all-gather | bytes 995328 | tf_op jit(solution)/shard_map/all_gather | solution.py:126
  74.8 26.4 %all_gather.41 = bf16[192,768]{0,1:T(8,128)(2,1)} all-gather(bf16[192,96]{0,1:T(8,128)(2,1)S(1)} %copy.64), channel_id=1, replica_groups=mesh['dp'=2,'hid'=4,'mod'=4] {'dp','hid'}, dimensions={1}, use_global_device_ids=true | all-gather | bytes 331776 | tf_op jit(solution)/shard_map/all_gather | solution.py:127
  112.3 10.4 %while.26 = (s32[]{:T(128)}, bf16[2,529,3,64]{1,3,2,0:T(8,128)(2,1)}, f32[2,3,529]{2,1,0:T(4,128)S(1)}, bf16[2,529,3,64]{1,3,2,0:T(8,128)(2,1)S(1)}, s32[2]{0:T(...) while((s32[]{:T(128)}, ...), condition=%wide.region_7.8_spmd, body=%wide.region_4.7_spmd.sunk | while | flops 224991088 | bytes 15301959 | solution.py:141
  128.4 36.4 %reduce-scatter.11.cloned.1.call-done = bf16[1058,192]{0,1:T(8,128)(2,1)} async-done(((bf16[1058,768]{0,1:T(8,128)(2,1)}), bf16[1058,192]{0,1:T(8,128)(2,1)}) %reduce-scatter.11.cloned.1.call-update) | async-done | bytes 406288 | tf_op jit(solution)/shard_map/reduce_scatter | solution.py:39
  166.0 17.1 %all-reduce.5 = (f32[1058]{0:T(1024)S(1)}, f32[1058]{0:T(1024)S(1)}) all-reduce(f32[1058]{0:T(1024)S(1)} %get-tuple-element.173, f32[1058]{0:T(1024)S(1)} %get-tuple-element.172), channel_id=1, replica_groups=mesh['dp'=2,'hid'=4,'mod'=4] {'mod'}, use_global_device_ids=true, to_apply=%region_12.13 | all-reduce | flops 2116 | bytes 16928 | tf_op jit(solution)/shard_map/psum | solution.py:31
  184.6 9.8 %convert_reduce_fusion.7 = f32[203136]{0:T(1024)} fusion(bf16[1,203136]{1,0:T(2,128)(2,1)} %param.21), kind=kLoop, calls=%fused_computation.138 | loop fusion | flops 203136 | bytes 1218816 | tf_op jit(solution)/shard_map/reshape | solution.py:157
  201.4 13.5 %all-gather.22.cloned.1.call-done = bf16[4,1058,192]{1,2,0:T(8,128)(2,1)} async-done(((bf16[1,1058,192]{1,2,0:T(8,128)(2,1)}), bf16[4,1058,192]{1,2,0:T(8,128)(2,1)}) %all-gather.22.cloned.1.call-update) | async-done | bytes 1625104 | tf_op jit(solution)/shard_map/all_gather | solution.py:45
  214.9 4.6 all-to-all-start
  221.7 28.3 %all-gather.26.cloned.1.call-done = bf16[4,1058,192]{1,2,0:T(8,128)(2,1)} async-done(((bf16[1,1058,192]{1,2,0:T(8,128)(2,1)}), bf16[4,1058,192]{1,2,0:T(8,128)(2,1)}) %all-gather.26.cloned.1.call-update) | async-done | bytes 1625104 | tf_op jit(solution)/shard_map/all_gather | solution.py:45
  249.9 10.9 %all-to-all-done = bf16[4,1058,192]{1,2,0:T(8,128)(2,1)} async-done(((bf16[4,1058,192]{1,2,0:T(8,128)(2,1)}), bf16[4,1058,192]{1,2,0:T(8,128)(2,1)}, u32[]{:S(2)}, u32[]{:S(2)}) %all-to-all-start) | async-done | bytes 1625120 | tf_op jit(solution)/shard_map/all_to_all | solution.py:59
  260.8 4.4 all-to-all-start.1
  269.3 29.0 %all-gather.16.cloned.1.call-done = bf16[768,768]{1,0:T(8,128)(2,1)} async-done(((bf16[192,768]{1,0:T(8,128)(2,1)}), bf16[768,768]{1,0:T(8,128)(2,1)}) %all-gather.16.cloned.1.call-update) | async-done | bytes 1179664 | tf_op jit(solution)/shard_map/all_gather | solution.py:148
  298.2 5.0 convolution_add_fusion
  303.2 35.8 %all-gather.18.cloned.1.call-done = bf16[768,768]{0,1:T(8,128)(2,1)} async-done(((bf16[768,192]{0,1:T(8,128)(2,1)}), bf16[768,768]{0,1:T(8,128)(2,1)}) %all-gather.18.cloned.1.call-update) | async-done | bytes 1179664 | tf_op jit(solution)/shard_map/all_gather | solution.py:149
  339.0 11.5 %fusion.68 = (bf16[1,1058,768]{2,1,0:T(8,128)(2,1)}, f32[1058,768]{1,0:T(8,128)S(1)}) fusion(f32[1058,768]{1,0:T(8,128)} %convolution_add_fusion, bf16[1058,768]{0,1:T(8,128)(2,1)} %bitcast.36, bf16[768,768]{0,1:T(8,128)(2,1)} %all-gather.18.cloned.1.call-done), kind=kOutput, calls=%fused_computation.91 | convolution fusion | flops 1306570752 | bytes 10930176 | tf_op jit(solution)/shard_map/rd,fd->rf/dot_general | solution.py:162
  353.7 117.0 %all-gather.24.cloned.1.call-done = bf16[4,1058,768]{2,1,0:T(8,128)(2,1)} async-done(((bf16[1,1058,768]{2,1,0:T(8,128)(2,1)}), bf16[4,1058,768]{2,1,0:T(8,128)(2,1)}) %all-gather.24.cloned.1.call-update) | async-done | bytes 6500368 | tf_op jit(solution)/shard_map/all_gather | solution.py:55
  470.7 7.3 reshape.159
  477.9 7.0 convolution_convert_fusion.1
  484.9 105.0 %all-gather.28.cloned.1.call-done = bf16[4,1058,768]{2,1,0:T(8,128)(2,1)} async-done(((bf16[1,1058,768]{2,1,0:T(8,128)(2,1)}), bf16[4,1058,768]{2,1,0:T(8,128)(2,1)}) %all-gather.28.cloned.1.call-update) | async-done | bytes 6500368 | tf_op jit(solution)/shard_map/all_gather | solution.py:55
  590.0 7.2 reshape.163
  597.2 6.3 convolution_convert_fusion
  605.4 87.2 %all-reduce.10.cloned.1.call-done = (bf16[4232,192]{0,1:T(8,128)(2,1)}, bf16[4232,192]{0,1:T(8,128)(2,1)}) async-done(((bf16[4232,192]{0,1:T(8,128)(2,1)}, bf16[4232,192]{0,1:T(8,128)(2,1)}), (bf16[4232,192]{0,1:T(8,128)(2,1)}, bf16[4232,192]{0,1:T(8,128)(2,1)})) %all-reduce.10.cloned.1.call-update) | async-done | bytes 3250192
  694.8 18.7 %all-reduce.4 = (f32[1058]{0:T(1024)S(1)}, f32[1058]{0:T(1024)S(1)}) all-reduce(f32[1058]{0:T(1024)S(1)} %get-tuple-element.165, f32[1058]{0:T(1024)S(1)} %get-tuple-element.166), channel_id=1, replica_groups=mesh['dp'=2,'hid'=4,'mod'=4] {'mod'}, use_global_device_ids=true, to_apply=%region_18.19 | all-reduce | flops 2116 | bytes 16928 | tf_op jit(solution)/shard_map/psum | solution.py:31
  725.0 4.8 convolution_convert_fusion.5
  739.1 4.8 convolution_convert_fusion.4
  745.1 9.4 %all-gather.20.cloned.1.call-done = bf16[1058,768]{0,1:T(8,128)(2,1)} async-done(((bf16[1058,192]{0,1:T(8,128)(2,1)}), bf16[1058,768]{0,1:T(8,128)(2,1)}) %all-gather.20.cloned.1.call-update) | async-done | bytes 1625104 | tf_op jit(solution)/shard_map/all_gather | solution.py:35
  761.6 17.2 %while.27 = (s32[]{:T(128)}, bf16[2,529,3,64]{1,3,2,0:T(8,128)(2,1)}, bf16[2,529,3,64]{1,3,2,0:T(8,128)(2,1)}, bf16[2,529,3,64]{1,3,2,0:T(8,128)(2,1)}, bf16[2,5...) while((s32[]{:T(128)}, ...), condition=%wide.region_21.22_spmd, body=%wide.region_19.21_spmd.sunk | while | flops 550394304 | bytes 41354848 | solution.py:181
  787.2 4.5 fusion.58
  833.6 16.6 %all-reduce.3 = (f32[1058]{0:T(1024)S(1)}, f32[1058]{0:T(1024)S(1)}) all-reduce(f32[1058]{0:T(1024)S(1)} %get-tuple-element.169, f32[1058]{0:T(1024)S(1)} %get-tuple-element.174), channel_id=1, replica_groups=mesh['dp'=2,'hid'=4,'mod'=4] {'mod'}, use_global_device_ids=true, to_apply=%region_26.27 | all-reduce | flops 2116 | bytes 16928 | tf_op jit(solution)/shard_map/psum | solution.py:31
  853.9 14.8 %psum.71 = f32[8,192]{1,0:T(8,128)} all-reduce(f32[8,192]{1,0:T(8,128)S(1)} %stack.39), channel_id=1, replica_groups=mesh['dp'=2,'hid'=4,'mod'=4] {'dp','hid'}, use_global_device_ids=true, to_apply=%region_41.42 | all-reduce | flops 1536 | bytes 12288 | tf_op jit(solution)/shard_map/psum | solution.py:212
  (278 shorter events, 159.2 us)
Async XLA Ops:
  7.2 94.1 %all-gather.14.cloned.1.call-start = ((), (), s32[]{:S(2)}) async-start(), calls=%async_computation.8 | async-start | bytes 2211840 | tf_op jit(solution)/shard_map/all_gather | solution.py:35
  17.5 57.4 %copy-start.39 = (f32[1,192]{1,0:T(1,128)}, f32[1,192]{1,0:T(1,128)S(1)}, u32[]{:S(2)}) copy-start(f32[1,192]{1,0:T(1,128)S(1)} %get-tuple-element.242) | copy-start | bytes 2308
  17.5 165.7 %copy-start.36 = (f32[1,192]{1,0:T(1,128)}, f32[1,192]{1,0:T(1,128)S(1)}, u32[]{:S(2)}) copy-start(f32[1,192]{1,0:T(1,128)S(1)} %get-tuple-element.240) | copy-start | bytes 2308
  39.0 125.7 %reduce-scatter.11.cloned.1.call-start = ((), (), s32[]{:S(2)}) async-start(), calls=%async_computation.9 | async-start | bytes 2211840 | tf_op jit(solution)/shard_map/reduce_scatter | solution.py:39
  122.7 43.3 %copy-start.29 = (f32[2,3,529]{2,1,0:T(4,128)}, f32[2,3,529]{2,1,0:T(4,128)S(1)}, u32[]{:S(2)}) copy-start(f32[2,3,529]{2,1,0:T(4,128)S(1)} %get-tuple-element.393) | copy-start | bytes 38092
  126.4 38.4 %copy-start.2 = (bf16[1058,192]{0,1:T(8,128)(2,1)}, bf16[1058,192]{0,1:T(8,128)(2,1)S(1)}, u32[]{:S(2)}) copy-start(bf16[1058,192]{0,1:T(8,128)(2,1)S(1)} %convert_element_type.170) | copy-start | bytes 1218820
  128.3 86.6 %all-gather.22.cloned.1.call-start = ((), (), s32[]{:S(2)}) async-start(), calls=%async_computation.14 | async-start | bytes 2211840 | tf_op jit(solution)/shard_map/all_gather | solution.py:45
  184.1 65.8 %all-gather.26.cloned.1.call-start = ((), (), s32[]{:S(2)}) async-start(), calls=%async_computation.16 | async-start | bytes 2211840 | tf_op jit(solution)/shard_map/all_gather | solution.py:45
  201.4 63.8 %copy-start.19 = (bf16[384,192]{0,1:T(8,128)(2,1)S(1)}, bf16[384,192]{0,1:T(8,128)(2,1)}, u32[]{:S(2)}) copy-start(bf16[384,192]{0,1:T(8,128)(2,1)} %param.18) | copy-start | bytes 442372
  214.9 45.9 %all-to-all-start = ((bf16[4,1058,192]{1,2,0:T(8,128)(2,1)}), bf16[4,1058,192]{1,2,0:T(8,128)(2,1)}, u32[]{:S(2)}, u32[]{:S(2)}) async-start(bf16[4,1058,192]{1,2,0:T(8,128)(2,1)} %all-gather.22.cloned.1.call-done), calls=%async_computation.1 | async-start | bytes 3538944 | tf_op jit(solution)/shard_map/all_to_all | solution.py:59
  219.5 78.8 %all-gather.16.cloned.1.call-start = ((), (), s32[]{:S(2)}) async-start(), calls=%async_computation.10 | async-start | bytes 1474560 | tf_op jit(solution)/shard_map/all_gather | solution.py:148
  221.6 45.8 %copy-start.46 = (bf16[384]{0:T(512)(128)(2,1)S(1)}, bf16[384]{0:T(512)(128)(2,1)}, u32[]{:S(2)}) copy-start(bf16[384]{0:T(512)(128)(2,1)} %param.19) | copy-start | bytes 2308
  260.8 78.2 %all-to-all-start.1 = ((bf16[4,1058,192]{1,2,0:T(8,128)(2,1)}), bf16[4,1058,192]{1,2,0:T(8,128)(2,1)}, u32[]{:S(2)}, u32[]{:S(2)}) async-start(bf16[4,1058,192]{1,2,0:T(8,128)(2,1)} %all-gather.26.cloned.1.call-done), calls=%async_computation.2 | async-start | bytes 3538944 | tf_op jit(solution)/shard_map/all_to_all | solution.py:59
  265.2 73.8 %all-gather.18.cloned.1.call-start = ((), (), s32[]{:S(2)}) async-start(), calls=%async_computation.11 | async-start | bytes 1474560 | tf_op jit(solution)/shard_map/all_gather | solution.py:149
  267.4 203.3 %all-gather.24.cloned.1.call-start = ((), (), s32[]{:S(2)}) async-start(), calls=%async_computation.15 | async-start | bytes 8171520 | tf_op jit(solution)/shard_map/all_gather | solution.py:55
  352.4 237.5 %all-gather.28.cloned.1.call-start = ((), (), s32[]{:S(2)}) async-start(), calls=%async_computation.17 | async-start | bytes 8171520 | tf_op jit(solution)/shard_map/all_gather | solution.py:55
  353.2 124.8 %copy-start.13 = (bf16[768,192]{0,1:T(8,128)(2,1)S(1)}, bf16[768,192]{0,1:T(8,128)(2,1)}, u32[]{:S(2)}) copy-start(bf16[768,192]{0,1:T(8,128)(2,1)} %all_gather.47) | copy-start | bytes 884740
  353.2 339.4 %all-reduce.10.cloned.1.call-start = ((), (), s32[]{:S(2)}) async-start(), calls=%async_computation.20 | async-start | bytes 6684672
  484.9 112.2 %copy-start.12 = (bf16[192,768]{1,0:T(8,128)(2,1)S(1)}, bf16[192,768]{1,0:T(8,128)(2,1)}, u32[]{:S(2)}) copy-start(bf16[192,768]{1,0:T(8,128)(2,1)} %all_gather.43) | copy-start | bytes 884740
  603.5 89.1 %copy-start.37 = (f32[1,192]{1,0:T(1,128)S(1)}, f32[1,192]{1,0:T(1,128)}, u32[]{:S(2)}) copy-start(f32[1,192]{1,0:T(1,128)} %copy-done.36) | copy-start | bytes 2308
  603.5 110.1 %copy-start.27 = (f32[1058]{0:T(1024)S(1)}, f32[1058]{0:T(1024)}, u32[]{:S(2)}) copy-start(f32[1058]{0:T(1024)} %copy-done.26) | copy-start | bytes 12700
  603.5 151.0 %all-gather.20.cloned.1.call-start = ((), (), s32[]{:S(2)}) async-start(), calls=%async_computation.12 | async-start | bytes 2211840 | tf_op jit(solution)/shard_map/all_gather | solution.py:35
  716.8 105.1 %reduce-scatter.15.cloned.1.call-start = ((), (), s32[]{:S(2)}) async-start(), calls=%async_computation.18 | async-start | bytes 589824
  730.8 92.1 %reduce-scatter.17.cloned.1.call-start = ((), (), s32[]{:S(2)}) async-start(), calls=%async_computation.19 | async-start | bytes 589824
  744.9 87.3 %reduce-scatter.13.cloned.1.call-start = ((), (), s32[]{:S(2)}) async-start(), calls=%async_computation.13 | async-start | bytes 2211840 | tf_op jit(solution)/shard_map/reduce_scatter | solution.py:39
  795.2 14.0 %all-to-all-start.3 = ((bf16[8,192,96]{2,1,0:T(8,128)(2,1)}), bf16[8,192,96]{2,1,0:T(8,128)(2,1)S(1)}, u32[]{:S(2)}, u32[]{:S(2)}) async-start(bf16[8,192,96]{2,1,0:T(8,128)(2,1)} %bitcast.171), calls=%async_computation.5 | async-start | bytes 786432 | tf_op jit(solution)/shard_map/all_to_all | solution.py:26
  809.1 20.6 %all-to-all-start.2 = ((bf16[8,3,96,192]{2,3,1,0:T(8,128)(2,1)}), bf16[8,3,96,192]{2,3,1,0:T(8,128)(2,1)}, u32[]{:S(2)}, u32[]{:S(2)}) async-start(bf16[8,3,96,192]{2,3,1,0:T(8,128)(2,1)} %bitcast.212), calls=%async_computation.4 | async-start | bytes 2359296 | tf_op jit(solution)/shard_map/all_to_all | solution.py:26
  821.2 29.1 %copy-start.28 = (f32[1058]{0:T(1024)S(1)}, f32[1058]{0:T(1024)}, u32[]{:S(2)}) copy-start(f32[1058]{0:T(1024)} %copy-done.26) | copy-start | bytes 12700
  821.2 29.1 %copy-start.32 = (f32[1058]{0:T(1024)S(1)}, f32[1058]{0:T(1024)}, u32[]{:S(2)}) copy-start(f32[1058]{0:T(1024)} %copy-done.31) | copy-start | bytes 12700
  821.2 29.1 %copy-start.35 = (f32[1058]{0:T(1024)S(1)}, f32[1058]{0:T(1024)}, u32[]{:S(2)}) copy-start(f32[1058]{0:T(1024)} %copy-done.34) | copy-start | bytes 12700
  821.2 29.1 %copy-start.38 = (f32[1,192]{1,0:T(1,128)S(1)}, f32[1,192]{1,0:T(1,128)}, u32[]{:S(2)}) copy-start(f32[1,192]{1,0:T(1,128)} %copy-done.36) | copy-start | bytes 2308
  821.2 29.1 %copy-start.43 = (f32[1,192]{1,0:T(1,128)S(1)}, f32[1,192]{1,0:T(1,128)}, u32[]{:S(2)}) copy-start(f32[1,192]{1,0:T(1,128)} %get-tuple-element.236) | copy-start | bytes 2308
  (45 other events, 373.6 us)
Sparse Core Ops, SparseCore 0:
  39.1 38.5 all-gather.13
  128.4 36.2 reduce-scatter.10
  184.3 30.5 all-gather.21
  217.3 32.5 all-gather.25
  251.4 46.7 all-gather.15
  299.7 39.1 all-gather.17
  352.5 118.0 all-gather.23
  472.3 117.5 all-gather.27
  603.6 88.9 all-reduce.9
  716.9 37.5 all-gather.19
  756.8 6.6 reduce-scatter.14
  765.6 8.9 reduce-scatter.16
  791.9 37.2 reduce-scatter.12
where the time goes:
time: 888 us; the launch traced here: 881 us
  waiting for transfers between devices  474 us (53%)
  blocking collectives  156 us (18%)
  local copies, waits for them, and re-layouts  87.6 us (10%)
  matrix products  72.3 us (8%)
  other arithmetic  55.9 us (6%)
  starting transfers between devices  18.5 us (2%)
  between operations  16.1 us (2%)
    all_gather x2, waiting for transfers between devices, hidden_rows(): return lax.all_gather(values, 'mod', axis=0, tiled=True)  222 us
    unnamed x16, waiting for transfers between devices  88.1 us
    psum x4, blocking collectives, feature_sums(): return lax.psum((first, second), 'mod')  72.9 us
    all_gather x2, waiting for transfers between devices, group_rows(): return lax.all_gather(values, 'hid', axis=0, tiled=True)  41.8 us
    reduce_scatter x2, waiting for transfers between devices, heads_sum(): lax.psum_scatter(values.astype(jnp.bfloat16), 'mod', scatter_dimension=1,...  36.4 us
    all_gather x1, waiting for transfers between devices, body(): lax.all_gather(w_out, 'mod', axis=1, tiled=True)  35.8 us
    all_gather x1, blocking collectives, body(): lax.all_gather(project_in, ('dp', 'hid'), axis=1, tiled=True)  33.3 us
    unnamed x100, local copies, waits for them, and re-layouts  31.9 us
  transfers between devices with their start and end apart: 17, of which 11 were waited for; matrix products, arithmetic and copies ran while one was open for 15% of the time, Pallas kernels for 0%

commit v1 on v0

v1 whole, which is shorter than its diff:
```python
from functools import partial

import jax
import jax.numpy as jnp
from jax import lax
from jax.sharding import PartitionSpec as P

D = 768
HEAD_DIM = 64
L = 529
FEAT = 192
HALF = 265
PAD = 272
ROWS = 2 * PAD
WIDE = 2 * FEAT
UNITS = D // 8
eps = 1e-06
bf16 = jnp.bfloat16
f32 = jnp.float32

X = [(0, 1), (1, 0), (2, 3), (3, 2)]
Y = [(0, 2), (2, 0), (1, 3), (3, 1)]


def dot(a, b, ca=1, cb=0):
    return lax.dot_general(a, b, (((ca,), (cb,)), ((), ())), preferred_element_type=f32)


def over_x(v):
    return lax.ppermute(v, "hid", X)


def over_y(v):
    return lax.ppermute(v, "hid", Y)


def over_core(v):
    n = lax.axis_size("dp")
    return lax.ppermute(v, "dp", [(i, i ^ 1) for i in range(n)])


def over_z(v, shift):
    n = lax.axis_size("mod")
    return lax.ppermute(v, "mod", [(i, (i + shift) % n) for i in range(n)])


def row_pairs(second, back):
    pairs = []
    for dp in range(lax.axis_size("dp")):
        for z in range(4):
            core = dp % 2
            parity = 1 - z % 2 if second else z % 2
            src, dst = dp * 4 + z, (dp - core + z // 2) * 4 + 2 * core + parity
            pairs.append((dst, src) if back else (src, dst))
    return pairs


def rows_there(v, second):
    return lax.ppermute(v, ("dp", "mod"), row_pairs(second, False))


def rows_back(v, second):
    return lax.ppermute(v, ("dp", "mod"), row_pairs(second, True))


def pack(pin, pout, ex, con, bias, vec):
    top = jnp.concatenate([pin[0], pin[1]], 1)
    low = jnp.concatenate([pin[2], pout.T], 1)
    hi = lax.reduce_precision(vec, 8, 7)
    lo = vec - hi
    vecs = jnp.pad(jnp.concatenate([hi, lo], 1).astype(bf16), ((0, 8), (0, 0)))
    attn = jnp.concatenate([top, low, vecs], 0)
    ffn = jnp.concatenate([ex, con.T, jnp.pad(bias[None], ((0, 15), (0, 0)))], 0)
    return attn, ffn


def natural(parts, z):
    order = (z - jnp.arange(4)) % 4
    return jnp.take(jnp.stack(parts), order, axis=0)


def norm(v, gain, shift):
    center = jnp.mean(v, 1, keepdims=True)
    moved = v - center
    inverse = lax.rsqrt(jnp.mean(moved * moved, 1, keepdims=True) + eps)
    normed = moved * inverse
    return normed, inverse, normed * gain + shift


def norm_back(grad, normed, inverse, gain):
    t = grad * gain
    return inverse * (t - jnp.mean(t, 1, keepdims=True) - normed * jnp.mean(t * normed, 1, keepdims=True))


def unflat(own1, own2, oth1, oth2, core, parity):
    def arrange(a, b):
        return jnp.where(parity == 0, a, b), jnp.where(parity == 0, b, a)

    own = arrange(own1, own2)
    oth = arrange(oth1, oth2)
    quarters = [jnp.where(core == 0, own[0], oth[0]), jnp.where(core == 0, own[1], oth[1]),
                jnp.where(core == 0, oth[0], own[0]), jnp.where(core == 0, oth[1], own[1])]
    quarters = [q.reshape(HALF, WIDE) for q in quarters]
    left = jnp.concatenate([q[:, :FEAT] for q in quarters], 1)
    right = jnp.concatenate([q[:, FEAT:] for q in quarters], 1)
    gap = ((0, PAD - HALF), (0, 0))
    return jnp.concatenate([jnp.pad(left, gap), jnp.pad(right, gap)], 0)


def reflat(v, core, parity):
    half = lax.dynamic_slice_in_dim(v, core * WIDE, WIDE, 1)
    q = []
    for i in range(2):
        part = half[:, i * FEAT : (i + 1) * FEAT]
        q.append(jnp.concatenate([part[:HALF], part[PAD : PAD + HALF]], 1).reshape(1, -1))
    return jnp.where(parity == 0, q[0], q[1]), jnp.where(parity == 0, q[1], q[0])


def heads_of(v, j):
    return [v[:, j * FEAT + h * HEAD_DIM : j * FEAT + (h + 1) * HEAD_DIM] for h in range(3)]


def attend(q, k, v, keep):
    logits = jnp.where(keep, dot(q, k, 1, 1) * 0.125, -1e30)
    top = jnp.max(logits, -1, keepdims=True)
    expo = jnp.exp(logits - top)
    total = jnp.sum(expo, -1, keepdims=True)
    mixed = dot((expo / total).astype(bf16), v)
    return mixed.astype(bf16), top + jnp.log(total)


def attend_back(q, k, v, keep, lse, grad):
    logits = jnp.where(keep, dot(q, k, 1, 1) * 0.125, -1e30)
    chance = jnp.exp(logits - lse)
    gchance = dot(grad, v, 1, 1)
    gv = dot(chance.astype(bf16), grad, 0, 0)
    inner = jnp.sum(chance * gchance, -1, keepdims=True)
    gl = (chance * (gchance - inner)).astype(bf16)
    gq = dot(gl, k) * 0.125
    gk = dot(gl, q, 0, 0) * 0.125
    return gq.astype(bf16), gk.astype(bf16), gv.astype(bf16)


def body(patches, visible, project_in, project_out, expand, contract, expand_bias, vectors, cotangent):
    n_dp = lax.axis_size("dp")
    more = n_dp // 2
    dp, hid, z = lax.axis_index("dp"), lax.axis_index("hid"), lax.axis_index("mod")
    core, parity = dp % 2, z % 2
    place = 4 * core + hid
    if more > 1:
        def mine_of(v, dim):
            whole = lax.all_gather(v, ("dp", "hid"), axis=dim, tiled=True)
            size = whole.shape[dim] // 8
            return lax.dynamic_slice_in_dim(whole, place * size, size, dim)

        project_in, project_out = mine_of(project_in, 1), mine_of(project_out, 1)
        expand, contract = mine_of(expand, 1), mine_of(contract, 0)
        expand_bias = mine_of(expand_bias, 0)

    a0, f0 = pack(project_in, project_out, expand, contract, expand_bias, vectors)
    a = [a0] + [over_z(a0, k) for k in (1, 2, 3)]
    size = HALF * WIDE
    jump = (HALF - 1) * WIDE

    def blocks(v):
        return (lax.dynamic_slice(v, (0, parity * jump), (1, size)),
                lax.dynamic_slice(v, (0, (1 - parity) * jump), (1, size)))

    pb, cb = blocks(patches), blocks(cotangent)
    first = rows_there(jnp.concatenate([pb[0], cb[0]], 0), False)
    second = rows_there(jnp.concatenate([pb[1], cb[1]], 0), True)
    both = jnp.concatenate([first, second], 0)
    other = over_core(both)
    counts = jnp.stack([visible, over_core(visible)])
    counts = jnp.where(core == 0, counts, counts[::-1]).reshape(4)
    count = counts[z]
    f = [f0] + [over_z(f0, k) for k in (1, 3, 2)]
    f = [f[0], f[1], f[3], f[2]]

    slot = jnp.arange(PAD)
    ids = jnp.concatenate([2 * slot - parity, 2 * slot + 1 - parity])
    real = (slot < HALF)
    real = jnp.concatenate([real, real]) & (ids >= 0) & (ids < L)
    keep = (real & (ids < count))
    keep_row, keep_col = keep[:, None], keep[None, :]

    x = unflat(both[0:1], both[2:3], other[0:1], other[2:3], core, parity)
    x = jnp.where(real[:, None], x, 0).astype(f32)
    grad_out = unflat(both[1:2], both[3:4], other[1:2], other[3:4], core, parity)
    grad_mlp = jnp.where(keep_row, grad_out, 0).astype(bf16)
    grad_out = grad_mlp.astype(f32)

    low = jnp.stack([a[0][:192], a[1][:192]])
    high = jnp.stack([a[2][:192], a[3][:192]])
    keeps, gives = jnp.where(core == 0, low, high), jnp.where(core == 0, high, low)
    got = over_core(gives)
    here = jnp.concatenate([keeps, got], 0)
    from_x, from_y = over_x(here), over_y(here)
    diag_a, diag_b = over_x(from_y[:2]), over_y(from_x[2:])
    fx, fy = over_x(f0), over_y(f0)
    f3 = jnp.stack(f[1:])
    fx3, fy3 = over_x(f3), over_y(f3)
    fd_a, fd_b = over_x(jnp.stack([fy, fy3[0]])), over_y(fx3[1:])
    by_hid = [here, from_x, from_y, jnp.concatenate([diag_a, diag_b], 0)]
    stacked = jnp.stack(by_hid)
    order_hid = jnp.arange(4) ^ hid
    stacked = jnp.take(stacked, order_hid, axis=0).reshape(4, 2, 2, 2, UNITS, WIDE)
    stacked = jnp.take(stacked, jnp.stack([core, 1 - core]), axis=1)
    w = stacked.transpose(2, 3, 1, 0, 4, 5).reshape(2, 2, D, WIDE)

    vq = natural([v[192:200] for v in a], z).astype(f32)
    vec = (vq[:, :, :FEAT] + vq[:, :, FEAT:]).transpose(1, 0, 2).reshape(8, D)
    slots = [(z - 2 * core - j) % 4 for j in range(2)]
    vec_slot = [(vq[s] if False else jnp.take(vq, s, axis=0)) for s in slots]
    vec_slot = [v[:, :FEAT] + v[:, FEAT:] for v in vec_slot]

    normed1, inv1, shifted1 = norm(x, vec[0:1], vec[1:2])
    attn_in = shifted1.astype(bf16)
    qs, ks, vs = [], [], []
    for j in range(2):
        qk = dot(attn_in, w[j, 0])
        vv = dot(attn_in, w[j, 1][:, :FEAT])
        qs += heads_of((qk[:, :FEAT] + vec_slot[j][2:3]).astype(bf16), 0)
        ks += heads_of(qk[:, FEAT:].astype(bf16), 0)
        vs += heads_of((vv + vec_slot[j][3:4]).astype(bf16), 0)
    outs = [attend(q, k, v, keep_col) for q, k, v in zip(qs, ks, vs)]
    mixed = [jnp.concatenate([o[0] for o in outs[3 * j : 3 * j + 3]], 1) for j in range(2)]
    part = sum(dot(mixed[j], w[j, 1][:, FEAT:], 1, 1) for j in range(2))
    resid = x + part + over_core(part.astype(bf16)).astype(f32) + vec[4:5]

    normed2, inv2, shifted2 = norm(resid, vec[5:6], vec[6:7])
    mlp_in = shifted2.astype(bf16)

    f_own = jnp.stack(f)
    f_x, f_y = jnp.concatenate([fx[None], fx3]), jnp.concatenate([fy[None], fy3])
    f_d = jnp.concatenate([fd_a, fd_b])
    mlp_out, gnm = 0.0, 0.0
    grads = []
    for piece in (f_own, f_x, f_y, f_d):
        nat = jnp.take(piece, (z - jnp.arange(4)) % 4, axis=0)
        ein, cout = nat[:, :FEAT].reshape(D, WIDE), nat[:, FEAT : 2 * FEAT].reshape(D, WIDE)
        bias = piece[0, 2 * FEAT : 2 * FEAT + 1].astype(f32)
        pre = dot(mlp_in, ein) + bias
        hidden = jax.nn.gelu(pre, approximate=False).astype(bf16)
        mlp_out += dot(hidden, cout, 1, 1)
        ghid = dot(grad_mlp, cout)
        gpre = jax.vjp(partial(jax.nn.gelu, approximate=False), pre)[1](ghid)[0].astype(bf16)
        gnm += dot(gpre, ein, 1, 1)
        g_in = dot(mlp_in, gpre, 0, 0)
        g_out = dot(grad_mlp, hidden, 0, 0)
        gb = jnp.pad(jnp.sum(gpre.astype(f32), 0, keepdims=True), ((0, 15), (0, 0)))
        grads.append((g_in.astype(bf16), g_out.astype(bf16), gb.astype(bf16)))

    mlp_sum = mlp_out + over_core(mlp_out.astype(bf16)).astype(f32)
    result = (keep_row * (resid + mlp_sum + vec[7:8])).astype(bf16)

    def add(u, v):
        return (u.astype(f32) + v.astype(f32)).astype(bf16)

    own, gx, gy, gd = [(jnp.concatenate([g[0], g[2]], 0), g[1]) for g in grads]
    rx, ry = over_x(gd[0]), over_y(gd[1])
    sx, sy = over_x(jnp.concatenate([gx[0], add(gx[1], ry)], 0)), over_y(jnp.concatenate([add(gy[0], rx), gy[1]], 0))
    total = jnp.concatenate(own, 0).astype(f32) + sx.astype(f32) + sy.astype(f32)

    def ffn_part(k):
        q = (z + k) % 4
        return jnp.concatenate([lax.dynamic_slice_in_dim(total, q * FEAT, FEAT, 0),
                                lax.dynamic_slice_in_dim(total, D + 16 + q * FEAT, FEAT, 0), total[D : D + 16]], 0)

    fsum = ffn_part(0)
    for k in (1, 2, 3):
        fsum += over_z(ffn_part(k).astype(bf16), k).astype(f32)
    expand_grad, contract_grad, bias_grad = fsum[:FEAT], fsum[FEAT : 2 * FEAT].T, fsum[2 * FEAT]

    gnm = gnm + over_core(gnm.astype(bf16)).astype(f32)
    grad_resid = grad_out + norm_back(gnm, normed2, inv2, vec[5:6])
    grad_branch = grad_resid.astype(bf16)
    gw, part, colsums = [], 0.0, []
    for j in range(2):
        gm = dot(grad_branch, w[j, 1][:, FEAT:]).astype(bf16)
        res = [attend_back(qs[3 * j + h], ks[3 * j + h], vs[3 * j + h], keep_col, outs[3 * j + h][1],
                           gm[:, h * HEAD_DIM : (h + 1) * HEAD_DIM]) for h in range(3)]
        gq, gk, gv = (jnp.concatenate([r[i] for r in res], 1) for i in range(3))
        gqk = jnp.concatenate([gq, gk], 1)
        part += dot(gqk, w[j, 0], 1, 1) + dot(gv, w[j, 1][:, :FEAT], 1, 1)
        gw.append((dot(attn_in, gqk, 0, 0),
                   jnp.concatenate([dot(attn_in, gv, 0, 0), dot(grad_branch, mixed[j], 0, 0)], 1)))
        colsums.append((jnp.sum(gq.astype(f32), 0), jnp.sum(gv.astype(f32), 0)))
    gna = part + over_core(part.astype(bf16)).astype(f32)
    grad_in = grad_resid + norm_back(gna, normed1, inv1, vec[0:1])

    zero = jnp.zeros((D,), f32)
    vg = jnp.stack([jnp.sum(gna * normed1, 0), jnp.sum(gna, 0), zero, zero, jnp.sum(grad_branch.astype(f32), 0),
                    jnp.sum(gnm * normed2, 0), jnp.sum(gnm, 0), jnp.sum(grad_out, 0)])
    vg = vg.reshape(8, 4, FEAT).transpose(1, 0, 2)
    pieces = []
    for j in range(2):
        v = jnp.take(vg, slots[j], axis=0)
        v = v.at[2].set(colsums[j][0]).at[3].set(colsums[j][1])
        v = jnp.pad(v, ((0, 8), (0, FEAT))).astype(bf16)
        pieces.append(v)
    blocks_of = []
    for i in range(4):
        four = []
        for p in range(2):
            for j in range(2):
                at = (4 * (core ^ p) + (hid ^ i)) * UNITS
                four.append(jnp.concatenate([lax.dynamic_slice_in_dim(g, at, UNITS, 0).astype(bf16) for g in gw[j]]
                                            + [pieces[j]], 0))
        blocks_of.append(jnp.stack(four))
    own, gx, gy, gd = blocks_of
    rx, ry = over_x(gd[:2]), over_y(gd[2:])
    sx = over_x(jnp.concatenate([gx[:2], add(gx[2:], ry)], 0))
    sy = over_y(jnp.concatenate([add(gy[:2], rx), gy[2:]], 0))
    total = own.astype(f32) + sx.astype(f32) + sy.astype(f32)
    got = over_core(total[2:].astype(bf16)).astype(f32)
    keeps = total[:2]
    slot_all = jnp.where(core == 0, jnp.concatenate([keeps, got], 0), jnp.concatenate([got, keeps], 0))
    asum = slot_all[0]
    for k in (1, 2, 3):
        asum += over_z(slot_all[k].astype(bf16), -k).astype(f32)
    in_grad = jnp.stack([asum[:UNITS, :FEAT], asum[:UNITS, FEAT:], asum[UNITS : 2 * UNITS, :FEAT]])
    out_grad = asum[UNITS : 2 * UNITS, FEAT:].T
    vector_grad = asum[2 * UNITS : 2 * UNITS + 8, :FEAT]

    def home(v):
        u1, u2 = reflat(v, core, parity)
        b1, b2 = rows_back(u1, False), rows_back(u2, True)
        s0, s1 = jnp.where(parity == 0, b1, b2), jnp.where(parity == 0, b2, b1)
        edge = HALF * WIDE - FEAT
        return jnp.concatenate([s0[:, :edge], s1[:, FEAT:]], 1)

    result = home(result)
    grad_input = home(grad_in.astype(bf16)).astype(f32)

    if more > 1:
        def spread(v, dim):
            whole = jnp.zeros(v.shape[:dim] + (8 * v.shape[dim],) + v.shape[dim + 1 :], f32)
            whole = lax.dynamic_update_slice_in_dim(whole, v, place * v.shape[dim], dim)
            return lax.psum_scatter(whole, ("dp", "hid"), scatter_dimension=dim, tiled=True)

        in_grad, out_grad = spread(in_grad, 1), spread(out_grad, 1)
        expand_grad, contract_grad, bias_grad = spread(expand_grad, 1), spread(contract_grad, 0), spread(bias_grad, 0)
        vector_grad = lax.psum(vector_grad, "dp") / 2
    return result, grad_input, in_grad, out_grad, expand_grad, contract_grad, bias_grad, vector_grad


def solution(mesh):
    rows = P("mod", ("dp", "hid"))
    in_specs = (rows, P(("dp", "hid")), P(None, ("dp", "hid"), "mod"), rows, rows, P(("dp", "hid"), "mod"),
                P(("dp", "hid")), P(None, "mod"), rows)
    out_specs = (rows, rows, P(None, ("dp", "hid"), "mod"), rows, rows, P(("dp", "hid"), "mod"),
                 P(("dp", "hid")), P(None, "mod"))
    return jax.shard_map(body, mesh=mesh, in_specs=in_specs, out_specs=out_specs, check_vma=False)
```

time: 888 us -> 397 us (0.45)
  waiting for transfers between devices: 474 us -> 47.3 us
  blocking collectives: 156 us -> 0 us
  starting transfers between devices: 18.5 us -> 111 us
  other arithmetic: 55.9 us -> 107 us
  local copies, waits for them, and re-layouts: 87.6 us -> 58.8 us
  between operations: 16.1 us -> 3.8 us
  matrix products: 72.3 us -> 62.1 us
    all_gather x8 -> x0, waiting for transfers between devices: 338 us -> none  [the longest x2 222 us: hidden_rows(): return lax.all_gather(values, 'mod', axis=0, tiled=True)]
    ppermute x0 -> x44, starting transfers between devices: none -> 111 us  [the longest x8 41.1 us: over_core(): return lax.ppermute(v, 'dp', [(i, i ^ 1) for i in range(n)])]
    unnamed x16 -> x0, waiting for transfers between devices: 88.1 us -> none
    psum x5 -> x0, blocking collectives: 87.7 us -> none  [the longest x4 72.9 us: feature_sums(): return lax.psum((first, second), 'mod')]
    all_gather x5 -> x0, blocking collectives: 65.8 us -> none  [the longest x1 33.3 us: body(): lax.all_gather(project_in, ('dp', 'hid'), axis=1, tiled=True)]
    ppermute x0 -> x44, waiting for transfers between devices: none -> 47.3 us  [the longest x12 18.2 us: over_z(): return lax.ppermute(v, 'mod', [(i, (i + shift) % n) for i in range(n)])]
    reduce_scatter x2 -> x0, waiting for transfers between devices: 36.4 us -> none  [heads_sum(): lax.psum_scatter(values.astype(jnp.bfloat16), 'mod', scatter_dimension=1,...]
    select_n x0 -> x14, other arithmetic: none -> 28.3 us  [the longest x1 17.3 us: unflat(): jnp.where(core == 0, own[1], oth[1])]
  transfers between devices with their start and end apart: 17 -> 44, of which waited for: 11 -> 7; matrix products, arithmetic and copies ran while one was open for 15% -> 47% of each run, Pallas kernels for 0% -> 0%
where the time goes in v1:
time: 397 us; the launch traced here: 390 us
  starting transfers between devices  111 us (28%)
  other arithmetic  107 us (27%)
  matrix products  62.1 us (16%)
  local copies, waits for them, and re-layouts  58.8 us (15%)
  waiting for transfers between devices  47.3 us (12%)
    dot_general x78, matrix products, dot(): lax.dot_general(a, b, (((ca,), (cb,)), ((), ())), preferred_element_type=...  62.1 us
    ppermute x8, starting transfers between devices, over_core(): return lax.ppermute(v, 'dp', [(i, i ^ 1) for i in range(n)])  41.1 us
    ppermute x12, starting transfers between devices, over_z(): return lax.ppermute(v, 'mod', [(i, (i + shift) % n) for i in range(n)])  39.7 us
    ppermute x12, waiting for transfers between devices, over_z(): return lax.ppermute(v, 'mod', [(i, (i + shift) % n) for i in range(n)])  18.2 us
    select_n x1, other arithmetic, unflat(): jnp.where(core == 0, own[1], oth[1])  17.3 us
    ppermute x9, waiting for transfers between devices, over_y(): return lax.ppermute(v, 'hid', Y)  16.6 us
    unnamed x280, local copies, waits for them, and re-layouts  16 us
    ppermute x9, starting transfers between devices, over_y(): return lax.ppermute(v, 'hid', Y)  10.6 us
  transfers between devices with their start and end apart: 44, of which 7 were waited for; matrix products, arithmetic and copies ran while one was open for 47% of the time, Pallas kernels for 0%

profile of v1, /device:TPU:0, one launch (start us, length us, event | category | flops | bytes accessed | tf_op | source)
XLA Modules:
  0.0 390.3 jit_solution(1026162114167605999)
XLA Ops:
  3.4 5.1 %collective-permute-start.6 = (bf16[208,384]{1,0:T(8,128)(2,1)S(1)}, bf16[208,384]{1,0:T(8,128)(2,1)S(1)}, u32[]{:S(2)}, u32[]{:S(2)}) collective-permute-start(bf16[208,384]{1,0:T(8,128)(2,1)S(1)} %pad_maximum_fusion.31), channel_id=1, source_target_pairs={{0,3},{1,0},{2,1},{3,2},{4,7},{5,4},{6,5},{7,6},{8,11},{9,8},{10,9... | collective-permute-start | bytes 479240 | tf_op jit(solution)/shard_map/ppermute | solution.py:44
  12.0 2.5 collective-permute-start.13
  29.3 6.7 %collective-permute-done.5 = bf16[208,384]{1,0:T(8,128)(2,1)} collective-permute-done((bf16[208,384]{1,0:T(8,128)(2,1)S(1)}, bf16[208,384]{1,0:T(8,128)(2,1)}, u32[]{:S(2)}, u32[]{:S(2)}) %collective-permute-start.5) | collective-permute-done | bytes 159776 | tf_op jit(solution)/shard_map/ppermute | solution.py:44
  41.3 20.0 %collective-permute-start.7 = (bf16[2,192,384]{2,1,0:T(8,128)(2,1)S(1)}, bf16[2,192,384]{2,1,0:T(8,128)(2,1)S(1)}, u32[]{:S(2)}, u32[]{:S(2)}) collective-permute-start(bf16[2,192,384]{2,1,0:T(8,128)(2,1)S(1)} %get-tuple-element.220), channel_id=1, source_target_pairs={{0,16},{16,0},{1,17},{17,1},{2,18},{18,2},{3,19},{19,3},{4,20},{20... | collective-permute-start | bytes 884744 | tf_op jit(solution)/shard_map/ppermute | solution.py:39
  72.8 2.2 pad_maximum_fusion.6
  77.6 11.0 %collective-permute-done.18 = bf16[400,384]{1,0:T(8,128)(2,1)} collective-permute-done((bf16[400,384]{1,0:T(8,128)(2,1)}, bf16[400,384]{1,0:T(8,128)(2,1)}, u32[]{:S(2)}, u32[]{:S(2)}) %collective-permute-start.18) | collective-permute-done | bytes 307232 | tf_op jit(solution)/shard_map/ppermute | solution.py:34
  96.9 17.3 %fusion.139 = (bf16[101760]{0:T(1024)(128)(2,1)S(1)}, bf16[101760]{0:T(1024)(128)(2,1)S(1)}, bf16[101760]{0:T(1024)(128)(2,1)S(1)}, bf16[101760]{0:T(1024)(128)(...) fusion(pred[]{:T(512)S(6)} %eq.19, ...), kind=kLoop, calls=%fused_computation.386 | loop fusion | flops 1628160 | bytes 3256322 | tf_op jit(solution)/shard_map/jit(_where)/select_n | solution.py:101
  137.7 2.4 gather_fusion.1
  142.2 2.4 gather_fusion.2
  160.4 2.5 pad_maximum_fusion.4
  162.9 3.1 gather_fusion.6
  166.0 2.7 broadcast_select_fusion.1
  174.1 2.5 multiply_convert_fusion.8
  178.9 2.5 multiply_convert_fusion.9
  184.6 2.9 multiply_convert_fusion.7
  192.1 2.5 multiply_convert_fusion.6
  204.0 2.1 fusion.350
  206.6 4.8 %collective-permute-done.37 = bf16[768,384]{1,0:T(8,128)(2,1)S(1)} collective-permute-done((bf16[768,384]{1,0:T(8,128)(2,1)S(1)}, bf16[768,384]{1,0:T(8,128)(2,1)S(1)}, u32[]{:S(2)}, u32[]{:S(2)}) %collective-permute-start.37) | collective-permute-done | bytes 589856 | tf_op jit(solution)/shard_map/ppermute | solution.py:34
  219.2 3.0 convert_reduce_fusion.2
  251.6 2.2 fusion.352
  266.1 5.5 %collective-permute-start.24 = (bf16[1,101760]{1,0:T(2,128)(2,1)S(1)}, bf16[1,101760]{1,0:T(2,128)(2,1)S(1)}, u32[]{:S(2)}, u32[]{:S(2)}) collective-permute-start(bf16[1,101760]{1,0:T(2,128)(2,1)S(1)} %bitcast.272), channel_id=1, source_target_pairs={{1,0},{0,1},{17,2},{16,3},{3,16},{2,17},{19,18},{18,19},{5,4},{4,5... | collective-permute-start | bytes 610568 | tf_op jit(solution)/shard_map/ppermute | solution.py:63
  273.7 6.1 %collective-permute-done.24 = bf16[1,101760]{1,0:T(2,128)(2,1)S(1)} collective-permute-done((bf16[1,101760]{1,0:T(2,128)(2,1)S(1)}, bf16[1,101760]{1,0:T(2,128)(2,1)S(1)}, u32[]{:S(2)}, u32[]{:S(2)}) %collective-permute-start.24) | collective-permute-done | bytes 203552 | tf_op jit(solution)/shard_map/ppermute | solution.py:63
  281.6 7.5 %pad_maximum_fusion.8 = bf16[1,203136]{1,0:T(2,128)(2,1)} fusion(bf16[1,101568]{1,0:T(2,128)(2,1)S(1)} %get-tuple-element.175, bf16[1,101568]{1,0:T(2,128)(2,1)S(1)} %get-tuple-element.174), kind=kLoop, calls=%fused_computation.327 | loop fusion | flops 812544 | bytes 812544 | tf_op jit(solution)/shard_map/concatenate | solution.py:331
  289.3 3.3 fusion.111
  301.2 2.1 convert_add_fusion.1
  304.7 15.3 %collective-permute-start.42 = (bf16[400,384]{1,0:T(8,128)(2,1)S(1)}, bf16[400,384]{1,0:T(8,128)(2,1)S(1)}, u32[]{:S(2)}, u32[]{:S(2)}) collective-permute-start(bf16[400,384]{1,0:T(8,128)(2,1)S(1)} %get-tuple-element.263), channel_id=1, source_target_pairs={{0,2},{1,3},{2,0},{3,1},{4,6},{5,7},{6,4},{7,5},{8,10},{9,11},{10,... | collective-permute-start | bytes 921608 | tf_op jit(solution)/shard_map/ppermute | solution.py:44
  325.1 6.3 %collective-permute-done.30 = bf16[4,208,384]{2,1,0:T(8,128)(2,1)S(1)} collective-permute-done((bf16[4,208,384]{2,1,0:T(8,128)(2,1)S(1)}, bf16[4,208,384]{2,1,0:T(8,128)(2,1)S(1)}, u32[]{:S(2)}, u32[]{:S(2)}) %collective-permute-start.30) | collective-permute-done | bytes 639008 | tf_op jit(solution)/shard_map/ppermute | solution.py:30
  332.6 20.5 %collective-permute-start.33 = (bf16[2,208,384]{2,1,0:T(8,128)(2,1)S(1)}, bf16[2,208,384]{2,1,0:T(8,128)(2,1)S(1)}, u32[]{:S(2)}, u32[]{:S(2)}) collective-permute-start(bf16[2,208,384]{2,1,0:T(8,128)(2,1)S(1)} %slice.1054), channel_id=1, source_target_pairs={{0,16},{16,0},{1,17},{17,1},{2,18},{18,2},{3,19},{19,3},{4,20},{20... | collective-permute-start | bytes 958472 | tf_op jit(solution)/shard_map/ppermute | solution.py:39
  353.0 7.4 %maximum_convert_fusion = f32[1,203136]{1,0:T(1,128)} fusion(bf16[1,101568]{1,0:T(2,128)(2,1)S(1)} %get-tuple-element.173, bf16[1,101568]{1,0:T(2,128)(2,1)S(1)} %get-tuple-element.172), kind=kLoop, calls=%fused_computation.328 | loop fusion | flops 812544 | bytes 1218816 | tf_op jit(solution)/shard_map/convert_element_type | solution.py:334
  361.9 4.3 %collective-permute-start.34 = (bf16[208,384]{1,0:T(8,128)(2,1)S(1)}, bf16[208,384]{1,0:T(8,128)(2,1)S(1)}, u32[]{:S(2)}, u32[]{:S(2)}) collective-permute-start(bf16[208,384]{1,0:T(8,128)(2,1)S(1)} %get-tuple-element.196), channel_id=1, source_target_pairs={{0,3},{1,0},{2,1},{3,2},{4,7},{5,4},{6,5},{7,6},{8,11},{9,8},{10,9... | collective-permute-start | bytes 479240 | tf_op jit(solution)/shard_map/ppermute | solution.py:44
  366.2 6.4 %collective-permute-start.35 = (bf16[208,384]{1,0:T(8,128)(2,1)S(1)}, bf16[208,384]{1,0:T(8,128)(2,1)S(1)}, u32[]{:S(2)}, u32[]{:S(2)}) collective-permute-start(bf16[208,384]{1,0:T(8,128)(2,1)S(1)} %get-tuple-element.198), channel_id=1, source_target_pairs={{0,2},{1,3},{2,0},{3,1},{4,6},{5,7},{6,4},{7,5},{8,10},{9,11},{10,... | collective-permute-start | bytes 479240 | tf_op jit(solution)/shard_map/ppermute | solution.py:44
  376.1 11.5 %collective-permute-done.35 = bf16[208,384]{1,0:T(8,128)(2,1)S(1)} collective-permute-done((bf16[208,384]{1,0:T(8,128)(2,1)S(1)}, bf16[208,384]{1,0:T(8,128)(2,1)S(1)}, u32[]{:S(2)}, u32[]{:S(2)}) %collective-permute-start.35) | collective-permute-done | bytes 159776 | tf_op jit(solution)/shard_map/ppermute | solution.py:44
  (627 shorter events, 190.0 us)
Async XLA Ops:
  3.4 24.4 %collective-permute-start.6 = (bf16[208,384]{1,0:T(8,128)(2,1)S(1)}, bf16[208,384]{1,0:T(8,128)(2,1)S(1)}, u32[]{:S(2)}, u32[]{:S(2)}) collective-permute-start(bf16[208,384]{1,0:T(8,128)(2,1)S(1)} %pad_maximum_fusion.31), channel_id=1, source_target_pairs={{0,3},{1,0},{2,1},{3,2},{4,7},{5,4},{6,5},{7,6},{8,11},{9,8},{10,9... | collective-permute-start | bytes 479240 | tf_op jit(solution)/shard_map/ppermute | solution.py:44
  8.5 27.5 %collective-permute-start.5 = (bf16[208,384]{1,0:T(8,128)(2,1)S(1)}, bf16[208,384]{1,0:T(8,128)(2,1)}, u32[]{:S(2)}, u32[]{:S(2)}) collective-permute-start(bf16[208,384]{1,0:T(8,128)(2,1)S(1)} %pad_maximum_fusion.31), channel_id=1, source_target_pairs={{0,2},{1,3},{2,0},{3,1},{4,6},{5,7},{6,4},{7,5},{8,10},{9,11},{10,... | collective-permute-start | bytes 479240 | tf_op jit(solution)/shard_map/ppermute | solution.py:44
  8.5 29.1 %collective-permute-start.4 = (bf16[208,384]{1,0:T(8,128)(2,1)S(1)}, bf16[208,384]{1,0:T(8,128)(2,1)}, u32[]{:S(2)}, u32[]{:S(2)}) collective-permute-start(bf16[208,384]{1,0:T(8,128)(2,1)S(1)} %pad_maximum_fusion.31), channel_id=1, source_target_pairs={{0,1},{1,2},{2,3},{3,0},{4,5},{5,6},{6,7},{7,4},{8,9},{9,10},{10,1... | collective-permute-start | bytes 479240 | tf_op jit(solution)/shard_map/ppermute | solution.py:44
  12.0 53.6 %collective-permute-start.13 = (bf16[400,384]{1,0:T(8,128)(2,1)}, bf16[400,384]{1,0:T(8,128)(2,1)S(1)}, u32[]{:S(2)}, u32[]{:S(2)}) collective-permute-start(bf16[400,384]{1,0:T(8,128)(2,1)} %get-tuple-element.238), channel_id=1, source_target_pairs={{0,1},{1,2},{2,3},{3,0},{4,5},{5,6},{6,7},{7,4},{8,9},{9,10},{10,1... | collective-permute-start | bytes 921608 | tf_op jit(solution)/shard_map/ppermute | solution.py:44
  23.6 43.5 %collective-permute-start.14 = (bf16[400,384]{1,0:T(8,128)(2,1)}, bf16[400,384]{1,0:T(8,128)(2,1)S(1)}, u32[]{:S(2)}, u32[]{:S(2)}) collective-permute-start(bf16[400,384]{1,0:T(8,128)(2,1)} %get-tuple-element.238), channel_id=1, source_target_pairs={{0,2},{1,3},{2,0},{3,1},{4,6},{5,7},{6,4},{7,5},{8,10},{9,11},{10,... | collective-permute-start | bytes 921608 | tf_op jit(solution)/shard_map/ppermute | solution.py:44
  27.8 41.0 %collective-permute-start.15 = (bf16[400,384]{1,0:T(8,128)(2,1)}, bf16[400,384]{1,0:T(8,128)(2,1)S(1)}, u32[]{:S(2)}, u32[]{:S(2)}) collective-permute-start(bf16[400,384]{1,0:T(8,128)(2,1)} %get-tuple-element.238), channel_id=1, source_target_pairs={{0,3},{1,0},{2,1},{3,2},{4,7},{5,4},{6,5},{7,6},{8,11},{9,8},{10,9... | collective-permute-start | bytes 921608 | tf_op jit(solution)/shard_map/ppermute | solution.py:44
  37.6 23.7 %collective-permute-start.2 = (bf16[2,101760]{1,0:T(2,128)(2,1)S(1)}, bf16[2,101760]{1,0:T(2,128)(2,1)S(1)}, u32[]{:S(2)}, u32[]{:S(2)}) collective-permute-start(bf16[2,101760]{1,0:T(2,128)(2,1)S(1)} %pad_maximum_fusion.17), channel_id=1, source_target_pairs={{0,1},{1,0},{2,17},{3,16},{16,3},{17,2},{18,19},{19,18},{4,5},{5,4... | collective-permute-start | bytes 1221128 | tf_op jit(solution)/shard_map/ppermute | solution.py:59
  41.3 21.8 %collective-permute-start.7 = (bf16[2,192,384]{2,1,0:T(8,128)(2,1)S(1)}, bf16[2,192,384]{2,1,0:T(8,128)(2,1)S(1)}, u32[]{:S(2)}, u32[]{:S(2)}) collective-permute-start(bf16[2,192,384]{2,1,0:T(8,128)(2,1)S(1)} %get-tuple-element.220), channel_id=1, source_target_pairs={{0,16},{16,0},{1,17},{17,1},{2,18},{18,2},{3,19},{19,3},{4,20},{20... | collective-permute-start | bytes 884744 | tf_op jit(solution)/shard_map/ppermute | solution.py:39
  63.1 33.8 %collective-permute-start.3 = (bf16[4,101760]{1,0:T(4,128)(2,1)}, bf16[4,101760]{1,0:T(4,128)(2,1)S(1)}, u32[]{:S(2)}, u32[]{:S(2)}) collective-permute-start(bf16[4,101760]{1,0:T(4,128)(2,1)} %pad_maximum_fusion.7), channel_id=1, source_target_pairs={{0,16},{16,0},{1,17},{17,1},{2,18},{18,2},{3,19},{19,3},{4,20},{20... | collective-permute-start | bytes 2442248 | tf_op jit(solution)/shard_map/ppermute | solution.py:39
  65.6 24.9 %collective-permute-start.9 = (bf16[4,192,384]{2,1,0:T(8,128)(2,1)}, bf16[4,192,384]{2,1,0:T(8,128)(2,1)}, u32[]{:S(2)}, u32[]{:S(2)}) collective-permute-start(bf16[4,192,384]{2,1,0:T(8,128)(2,1)} %get-tuple-element.218), channel_id=1, source_target_pairs={{0,8},{8,0},{4,12},{12,4},{1,9},{9,1},{5,13},{13,5},{2,10},{10,2},... | collective-permute-start | bytes 1769480 | tf_op jit(solution)/shard_map/ppermute | solution.py:34
  67.1 26.6 %collective-permute-start.8 = (bf16[4,192,384]{2,1,0:T(8,128)(2,1)}, bf16[4,192,384]{2,1,0:T(8,128)(2,1)}, u32[]{:S(2)}, u32[]{:S(2)}) collective-permute-start(bf16[4,192,384]{2,1,0:T(8,128)(2,1)} %get-tuple-element.218), channel_id=1, source_target_pairs={{0,4},{4,0},{8,12},{12,8},{1,5},{5,1},{9,13},{13,9},{2,6},{6,2},{1... | collective-permute-start | bytes 1769480 | tf_op jit(solution)/shard_map/ppermute | solution.py:30
  68.8 19.8 %collective-permute-start.18 = (bf16[400,384]{1,0:T(8,128)(2,1)}, bf16[400,384]{1,0:T(8,128)(2,1)}, u32[]{:S(2)}, u32[]{:S(2)}) collective-permute-start(bf16[400,384]{1,0:T(8,128)(2,1)} %get-tuple-element.238), channel_id=1, source_target_pairs={{0,8},{8,0},{4,12},{12,4},{1,9},{9,1},{5,13},{13,5},{2,10},{10,2},... | collective-permute-start | bytes 921608 | tf_op jit(solution)/shard_map/ppermute | solution.py:34
  75.0 47.8 %collective-permute-start.19 = (bf16[3,400,384]{2,1,0:T(8,128)(2,1)}, bf16[3,400,384]{2,1,0:T(8,128)(2,1)}, u32[]{:S(2)}, u32[]{:S(2)}) collective-permute-start(bf16[3,400,384]{2,1,0:T(8,128)(2,1)} %pad_maximum_fusion.6), channel_id=1, source_target_pairs={{0,8},{8,0},{4,12},{12,4},{1,9},{9,1},{5,13},{13,5},{2,10},{10,2},... | collective-permute-start | bytes 2764808 | tf_op jit(solution)/shard_map/ppermute | solution.py:34
  88.6 37.6 %collective-permute-start.17 = (bf16[3,400,384]{2,1,0:T(8,128)(2,1)}, bf16[3,400,384]{2,1,0:T(8,128)(2,1)}, u32[]{:S(2)}, u32[]{:S(2)}) collective-permute-start(bf16[3,400,384]{2,1,0:T(8,128)(2,1)} %pad_maximum_fusion.6), channel_id=1, source_target_pairs={{0,4},{4,0},{8,12},{12,8},{1,5},{5,1},{9,13},{13,9},{2,6},{6,2},{1... | collective-permute-start | bytes 2764808 | tf_op jit(solution)/shard_map/ppermute | solution.py:30
  92.2 42.8 %collective-permute-start.10 = (bf16[2,192,384]{2,1,0:T(8,128)(2,1)}, bf16[2,192,384]{2,1,0:T(8,128)(2,1)}, u32[]{:S(2)}, u32[]{:S(2)}) collective-permute-start(bf16[2,192,384]{2,1,0:T(8,128)(2,1)} %slice.682), channel_id=1, source_target_pairs={{0,4},{4,0},{8,12},{12,8},{1,5},{5,1},{9,13},{13,9},{2,6},{6,2},{1... | collective-permute-start | bytes 884744 | tf_op jit(solution)/shard_map/ppermute | solution.py:30
  95.4 39.6 %collective-permute-start.11 = (bf16[2,192,384]{2,1,0:T(8,128)(2,1)}, bf16[2,192,384]{2,1,0:T(8,128)(2,1)}, u32[]{:S(2)}, u32[]{:S(2)}) collective-permute-start(bf16[2,192,384]{2,1,0:T(8,128)(2,1)} %slice.683), channel_id=1, source_target_pairs={{0,8},{8,0},{4,12},{12,4},{1,9},{9,1},{5,13},{13,5},{2,10},{10,2},... | collective-permute-start | bytes 884744 | tf_op jit(solution)/shard_map/ppermute | solution.py:34
  125.7 34.7 %collective-permute-start.20 = (bf16[2,400,384]{2,1,0:T(8,128)(2,1)}, bf16[2,400,384]{2,1,0:T(8,128)(2,1)}, u32[]{:S(2)}, u32[]{:S(2)}) collective-permute-start(bf16[2,400,384]{2,1,0:T(8,128)(2,1)} %pad_maximum_fusion.11), channel_id=1, source_target_pairs={{0,4},{4,0},{8,12},{12,8},{1,5},{5,1},{9,13},{13,9},{2,6},{6,2},{1... | collective-permute-start | bytes 1843208 | tf_op jit(solution)/shard_map/ppermute | solution.py:30
  128.2 32.2 %collective-permute-start.21 = (bf16[2,400,384]{2,1,0:T(8,128)(2,1)}, bf16[2,400,384]{2,1,0:T(8,128)(2,1)}, u32[]{:S(2)}, u32[]{:S(2)}) collective-permute-start(bf16[2,400,384]{2,1,0:T(8,128)(2,1)} %slice.733), channel_id=1, source_target_pairs={{0,8},{8,0},{4,12},{12,4},{1,9},{9,1},{5,13},{13,5},{2,10},{10,2},... | collective-permute-start | bytes 1843208 | tf_op jit(solution)/shard_map/ppermute | solution.py:34
  198.9 16.1 %collective-permute-start.39 = (bf16[784,384]{1,0:T(8,128)(2,1)S(1)}, bf16[784,384]{1,0:T(8,128)(2,1)S(1)}, u32[]{:S(2)}, u32[]{:S(2)}) collective-permute-start(bf16[784,384]{1,0:T(8,128)(2,1)S(1)} %fusion.116), channel_id=1, source_target_pairs={{0,4},{4,0},{8,12},{12,8},{1,5},{5,1},{9,13},{13,9},{2,6},{6,2},{1... | collective-permute-start | bytes 1806344 | tf_op jit(solution)/shard_map/ppermute | solution.py:30
  201.7 16.1 %collective-permute-start.25 = (bf16[544,768]{1,0:T(8,128)(2,1)S(1)}, bf16[544,768]{1,0:T(8,128)(2,1)S(1)}, u32[]{:S(2)}, u32[]{:S(2)}) collective-permute-start(bf16[544,768]{1,0:T(8,128)(2,1)S(1)} %get-tuple-element.316), channel_id=1, source_target_pairs={{0,16},{16,0},{1,17},{17,1},{2,18},{18,2},{3,19},{19,3},{4,20},{20... | collective-permute-start | bytes 2506760 | tf_op jit(solution)/shard_map/ppermute | solution.py:39
  206.1 56.4 %collective-permute-start.22 = (bf16[544,768]{1,0:T(8,128)(2,1)}, bf16[544,768]{1,0:T(8,128)(2,1)}, u32[]{:S(2)}, u32[]{:S(2)}) collective-permute-start(bf16[544,768]{1,0:T(8,128)(2,1)} %get-tuple-element.314), channel_id=1, source_target_pairs={{0,16},{16,0},{1,17},{17,1},{2,18},{18,2},{3,19},{19,3},{4,20},{20... | collective-permute-start | bytes 2506760 | tf_op jit(solution)/shard_map/ppermute | solution.py:39
  213.4 85.7 %collective-permute-start.38 = (bf16[1552,384]{1,0:T(8,128)(2,1)}, bf16[1552,384]{1,0:T(8,128)(2,1)}, u32[]{:S(2)}, u32[]{:S(2)}) collective-permute-start(bf16[1552,384]{1,0:T(8,128)(2,1)} %fusion.28), channel_id=1, source_target_pairs={{0,4},{4,0},{8,12},{12,8},{1,5},{5,1},{9,13},{13,9},{2,6},{6,2},{1... | collective-permute-start | bytes 3575816 | tf_op jit(solution)/shard_map/ppermute | solution.py:30
  216.3 84.9 %collective-permute-start.40 = (bf16[1552,384]{1,0:T(8,128)(2,1)}, bf16[1552,384]{1,0:T(8,128)(2,1)}, u32[]{:S(2)}, u32[]{:S(2)}) collective-permute-start(bf16[1552,384]{1,0:T(8,128)(2,1)} %pad_maximum_fusion.5), channel_id=1, source_target_pairs={{0,8},{8,0},{4,12},{12,4},{1,9},{9,1},{5,13},{13,5},{2,10},{10,2},... | collective-permute-start | bytes 3575816 | tf_op jit(solution)/shard_map/ppermute | solution.py:34
  254.5 34.6 %collective-permute-start.26 = (bf16[544,768]{1,0:T(8,128)(2,1)}, bf16[544,768]{1,0:T(8,128)(2,1)}, u32[]{:S(2)}, u32[]{:S(2)}) collective-permute-start(bf16[544,768]{1,0:T(8,128)(2,1)} %get-tuple-element.342), channel_id=1, source_target_pairs={{0,16},{16,0},{1,17},{17,1},{2,18},{18,2},{3,19},{19,3},{4,20},{20... | collective-permute-start | bytes 2506760 | tf_op jit(solution)/shard_map/ppermute | solution.py:39
  295.8 24.3 %collective-permute-start.31 = (bf16[2,208,384]{2,1,0:T(8,128)(2,1)S(1)}, bf16[2,208,384]{2,1,0:T(8,128)(2,1)S(1)}, u32[]{:S(2)}, u32[]{:S(2)}) collective-permute-start(bf16[2,208,384]{2,1,0:T(8,128)(2,1)S(1)} %pad_maximum_fusion.19), channel_id=1, source_target_pairs={{0,4},{4,0},{8,12},{12,8},{1,5},{5,1},{9,13},{13,9},{2,6},{6,2},{1... | collective-permute-start | bytes 958472 | tf_op jit(solution)/shard_map/ppermute | solution.py:30
  298.1 22.9 %collective-permute-start.27 = (bf16[1,101760]{1,0:T(2,128)(2,1)S(1)}, bf16[1,101760]{1,0:T(2,128)(2,1)S(1)}, u32[]{:S(2)}, u32[]{:S(2)}) collective-permute-start(bf16[1,101760]{1,0:T(2,128)(2,1)S(1)} %bitcast.270), channel_id=1, source_target_pairs={{0,0},{1,1},{16,2},{17,3},{2,16},{3,17},{18,18},{19,19},{4,4},{5,5... | collective-permute-start | bytes 610568 | tf_op jit(solution)/shard_map/ppermute | solution.py:63
  299.1 22.8 %collective-permute-start.28 = (bf16[1,101760]{1,0:T(2,128)(2,1)S(1)}, bf16[1,101760]{1,0:T(2,128)(2,1)S(1)}, u32[]{:S(2)}, u32[]{:S(2)}) collective-permute-start(bf16[1,101760]{1,0:T(2,128)(2,1)S(1)} %bitcast.269), channel_id=1, source_target_pairs={{1,0},{0,1},{17,2},{16,3},{3,16},{2,17},{19,18},{18,19},{5,4},{4,5... | collective-permute-start | bytes 610568 | tf_op jit(solution)/shard_map/ppermute | solution.py:63
  303.5 56.9 %collective-permute-start.41 = (bf16[400,384]{1,0:T(8,128)(2,1)S(1)}, bf16[400,384]{1,0:T(8,128)(2,1)S(1)}, u32[]{:S(2)}, u32[]{:S(2)}) collective-permute-start(bf16[400,384]{1,0:T(8,128)(2,1)S(1)} %get-tuple-element.262), channel_id=1, source_target_pairs={{0,1},{1,2},{2,3},{3,0},{4,5},{5,6},{6,7},{7,4},{8,9},{9,10},{10,1... | collective-permute-start | bytes 921608 | tf_op jit(solution)/shard_map/ppermute | solution.py:44
  304.7 55.7 %collective-permute-start.42 = (bf16[400,384]{1,0:T(8,128)(2,1)S(1)}, bf16[400,384]{1,0:T(8,128)(2,1)S(1)}, u32[]{:S(2)}, u32[]{:S(2)}) collective-permute-start(bf16[400,384]{1,0:T(8,128)(2,1)S(1)} %get-tuple-element.263), channel_id=1, source_target_pairs={{0,2},{1,3},{2,0},{3,1},{4,6},{5,7},{6,4},{7,5},{8,10},{9,11},{10,... | collective-permute-start | bytes 921608 | tf_op jit(solution)/shard_map/ppermute | solution.py:44
  320.1 40.3 %collective-permute-start.43 = (bf16[400,384]{1,0:T(8,128)(2,1)S(1)}, bf16[400,384]{1,0:T(8,128)(2,1)S(1)}, u32[]{:S(2)}, u32[]{:S(2)}) collective-permute-start(bf16[400,384]{1,0:T(8,128)(2,1)S(1)} %get-tuple-element.264), channel_id=1, source_target_pairs={{0,3},{1,0},{2,1},{3,2},{4,7},{5,4},{6,5},{7,6},{8,11},{9,8},{10,9... | collective-permute-start | bytes 921608 | tf_op jit(solution)/shard_map/ppermute | solution.py:44
  332.6 28.0 %collective-permute-start.33 = (bf16[2,208,384]{2,1,0:T(8,128)(2,1)S(1)}, bf16[2,208,384]{2,1,0:T(8,128)(2,1)S(1)}, u32[]{:S(2)}, u32[]{:S(2)}) collective-permute-start(bf16[2,208,384]{2,1,0:T(8,128)(2,1)S(1)} %slice.1054), channel_id=1, source_target_pairs={{0,16},{16,0},{1,17},{17,1},{2,18},{18,2},{3,19},{19,3},{4,20},{20... | collective-permute-start | bytes 958472 | tf_op jit(solution)/shard_map/ppermute | solution.py:39
  366.2 21.4 %collective-permute-start.35 = (bf16[208,384]{1,0:T(8,128)(2,1)S(1)}, bf16[208,384]{1,0:T(8,128)(2,1)S(1)}, u32[]{:S(2)}, u32[]{:S(2)}) collective-permute-start(bf16[208,384]{1,0:T(8,128)(2,1)S(1)} %get-tuple-element.198), channel_id=1, source_target_pairs={{0,2},{1,3},{2,0},{3,1},{4,6},{5,7},{6,4},{7,5},{8,10},{9,11},{10,... | collective-permute-start | bytes 479240 | tf_op jit(solution)/shard_map/ppermute | solution.py:44
  (151 other events, 923.8 us)

commit v2 on v1

v2 whole, which is shorter than its diff:
```python
import jax
import jax.numpy as jnp
from jax import lax
from jax.experimental import pallas as pl
from jax.experimental.pallas import tpu as pltpu
from jax.sharding import PartitionSpec as P

D = 768
HEAD_DIM = 64
L = 529
FEAT = 192
HALF = 265
PAD = 272
ROWS = 2 * PAD
WIDE = 2 * FEAT
UNITS = D // 8
APIECE = 2 * UNITS + 16
FPIECE = 2 * FEAT + 16
eps = 1e-06
bf16 = jnp.bfloat16
f32 = jnp.float32

X = [(0, 1), (1, 0), (2, 3), (3, 2)]
Y = [(0, 2), (2, 0), (1, 3), (3, 1)]


def dot(a, b, ca=1, cb=0):
    return lax.dot_general(a, b, (((ca,), (cb,)), ((), ())), preferred_element_type=f32)


def over_x(v):
    return lax.ppermute(v, "hid", X)


def over_y(v):
    return lax.ppermute(v, "hid", Y)


def over_core(v):
    n = lax.axis_size("dp")
    return lax.ppermute(v, "dp", [(i, i ^ 1) for i in range(n)])


def over_z(v, shift):
    n = lax.axis_size("mod")
    return lax.ppermute(v, "mod", [(i, (i + shift) % n) for i in range(n)])


def row_pairs(second, back):
    pairs = []
    for dp in range(lax.axis_size("dp")):
        for z in range(4):
            core = dp % 2
            parity = 1 - z % 2 if second else z % 2
            src, dst = dp * 4 + z, (dp - core + z // 2) * 4 + 2 * core + parity
            pairs.append((dst, src) if back else (src, dst))
    return pairs


def rows_there(v, second):
    return lax.ppermute(v, ("dp", "mod"), row_pairs(second, False))


def rows_back(v, second):
    return lax.ppermute(v, ("dp", "mod"), row_pairs(second, True))


VM = pl.BlockSpec(memory_space=pltpu.VMEM)
SM = pl.BlockSpec(memory_space=pltpu.SMEM)


def call(kernel, outs, scal, *args, flops=0, limit=48, scratch=(), name=None):
    outs = [jax.ShapeDtypeStruct(s, t) for s, t in outs]
    size = sum(a.size * a.dtype.itemsize for a in args) + sum(o.size * o.dtype.itemsize for o in outs)
    single = len(outs) == 1
    ins = ([] if scal is None else [SM]) + [VM] * len(args)
    if scal is not None:
        args = (scal,) + args
    return pl.pallas_call(
        kernel,
        out_shape=outs[0] if single else outs,
        in_specs=ins,
        out_specs=VM if single else [VM] * len(outs),
        scratch_shapes=list(scratch),
        cost_estimate=pl.CostEstimate(flops=int(flops), bytes_accessed=int(size), transcendentals=0),
        compiler_params=pltpu.CompilerParams(vmem_limit_bytes=limit * 2**20),
        name=name,
    )(*args)


def k_pack(pin, pout, ex, con, bias, vec, attn, ffn):
    u = UNITS
    attn[0:u, 0:FEAT] = pin[0]
    attn[0:u, FEAT:WIDE] = pin[1]
    attn[u : 2 * u, 0:FEAT] = pin[2]
    attn[u : 2 * u, FEAT:WIDE] = pout[...].astype(f32).T.astype(bf16)
    v = vec[...]
    hi = v.astype(bf16)
    lo = (v - hi.astype(f32)).astype(bf16)
    both = jnp.concatenate([hi.astype(f32), lo.astype(f32)], 1)
    attn[2 * u : APIECE, :] = jnp.concatenate([both, jnp.zeros_like(both)], 0).astype(bf16)
    ffn[0:FEAT, :] = ex[...]
    ffn[FEAT:WIDE, :] = con[...].astype(f32).T.astype(bf16)
    ffn[WIDE:FPIECE, :] = jnp.broadcast_to(bias[...].astype(f32), (16, WIDE)).astype(bf16)


def k_in(scal, p, c, p1, p2, c1, c2):
    even = scal[2] % 2 == 0

    @pl.when(even)
    def _():
        p1[...] = p[0:HALF, 0, :]
        p2[...] = p[HALF - 1 : L, 0, :]
        c1[...] = c[0:HALF, 0, :]
        c2[...] = c[HALF - 1 : L, 0, :]

    @pl.when(jnp.logical_not(even))
    def _():
        p2[...] = p[0:HALF, 0, :]
        p1[...] = p[HALF - 1 : L, 0, :]
        c2[...] = c[0:HALF, 0, :]
        c1[...] = c[HALF - 1 : L, 0, :]


def row_ids(parity, shape, dim):
    place = lax.broadcasted_iota(jnp.int32, shape, dim)
    right = place >= PAD
    slot = jnp.where(right, place - PAD, place)
    ids = 2 * slot - parity + jnp.where(right, 1, 0)
    real = (slot < HALF) & (ids >= 0) & (ids < L)
    return real, ids


def kept_rows(scal, shape=(ROWS, 1), dim=0):
    real, ids = row_ids(scal[2] % 2, shape, dim)
    return real & (ids < scal[3])


def assemble(scal, own1, own2, oth1, oth2, out):
    core, even = scal[0], scal[2] % 2 == 0
    a, b, c, d = (r[...].astype(f32) for r in (own1, own2, oth1, oth2))
    own = jnp.where(even, a, b), jnp.where(even, b, a)
    oth = jnp.where(even, c, d), jnp.where(even, d, c)
    first = core == 0
    for q in range(4):
        mine, theirs = (own, oth) if q < 2 else (oth, own)
        v = jnp.where(first, mine[q % 2], theirs[q % 2])
        out[0:HALF, q * FEAT : (q + 1) * FEAT] = v[:, :FEAT]
        out[PAD : PAD + HALF, q * FEAT : (q + 1) * FEAT] = v[:, FEAT:]


def norm(v, gain, shift):
    moved = v - jnp.mean(v, 1, keepdims=True)
    inverse = lax.rsqrt(jnp.mean(moved * moved, 1, keepdims=True) + eps)
    normed = moved * inverse
    return normed, inverse, normed * gain + shift


def norm_back(grad, normed, inverse, gain):
    t = grad * gain
    return inverse * (t - jnp.mean(t, 1, keepdims=True) - normed * jnp.mean(t * normed, 1, keepdims=True))


def vec_block(refs, k):
    v = refs[0][2 * UNITS : APIECE, :].astype(f32)
    for i in (1, 2, 3):
        v = jnp.where(k == i, refs[i][2 * UNITS : APIECE, :].astype(f32), v)
    return v[0:8, :FEAT] + v[0:8, FEAT:]


def k_norm1(scal, own1, own2, oth1, oth2, a0, a1, a2, a3, x, ain, ain_t, vec, slots, buf):
    core, z = scal[0], scal[2]
    refs = (a0, a1, a2, a3)
    for q in range(4):
        vec[:, q * FEAT : (q + 1) * FEAT] = vec_block(refs, (z - q + 4) % 4)
    for j in range(2):
        slots[j] = vec_block(refs, 2 * core + j)
    assemble(scal, own1, own2, oth1, oth2, buf)
    real, _ = row_ids(z % 2, (ROWS, 1), 0)
    v = jnp.where(real, buf[...], 0.0)
    x[...] = v.astype(bf16)
    low = norm(v, vec[0:1, :], vec[1:2, :])[2].astype(bf16)
    ain[...] = low
    ain_t[...] = low.T


def k_give(scal, a0, a1, a2, a3, keeps, gives):
    first = scal[0] == 0
    for j, (lo, hi) in enumerate(((a0, a2), (a1, a3))):
        u, v = lo[0 : 2 * UNITS, :], hi[0 : 2 * UNITS, :]
        keeps[j] = jnp.where(first, u, v)
        gives[j] = jnp.where(first, v, u)


def k_attn(scal, ain, h_own, h_got, fx, fy, da, db, slots, w, q, k, v, lse, mixed, part, part_low, qt, vt, mt):
    core, hid = scal[0], scal[1]
    for i in range(4):
        for p in range(2):
            for j in range(2):
                src = ((h_own, h_got)[p], None, None, None)[i]
                if i == 0:
                    src = (h_own, h_got)[p][j]
                elif i == 3:
                    src = (da, db)[p][j]
                else:
                    src = (fx, fy)[i - 1][2 * p + j]
                at = pl.multiple_of((4 * (core ^ p) + (hid ^ i)) * UNITS, 32)
                w[j, 0, pl.ds(at, UNITS), :] = src[0:UNITS]
                w[j, 1, pl.ds(at, UNITS), :] = src[UNITS : 2 * UNITS]
    keep = kept_rows(scal)
    lane = lax.broadcasted_iota(jnp.int32, (1, FEAT), 1) // HEAD_DIM
    for j in range(2):
        qk = dot(ain[...], w[j, 0])
        qj = (qk[:, :FEAT] + slots[j, 2:3, :]).astype(bf16) * jnp.asarray(0.125, bf16)
        q[j] = qj
        qt[j] = qj.T
        k[j] = qk[:, FEAT:].astype(bf16)
        vj = (dot(ain[...], w[j, 1, :, 0:FEAT]) + slots[j, 3:4, :]).astype(bf16)
        v[j] = vj
        vt[j] = vj.T
    lse[...] = jnp.zeros_like(lse)
    for j in range(2):
        for h in range(3):
            kh = jnp.where(lane == h, k[j], jnp.zeros((), bf16))
            logits = jnp.where(keep, dot(kh, qt[j]), -1e30)
            top = jnp.max(logits, 0, keepdims=True)
            expo = jnp.exp(logits - top)
            total = jnp.sum(expo, 0, keepdims=True)
            chance = (expo * (1.0 / total)).astype(bf16)
            rows = slice(h * HEAD_DIM, (h + 1) * HEAD_DIM)
            mt[j, rows, :] = dot(vt[j, rows, :], chance)
            lse[3 * j + h : 3 * j + h + 1, :] = top + jnp.log(total)
    total = 0.0
    for j in range(2):
        mj = mt[j].T.astype(bf16)
        mixed[j] = mj
        total += dot(mj, w[j, 1, :, FEAT:WIDE], 1, 1)
    part[...] = total
    part_low[...] = total.astype(bf16)


def k_norm2(scal, x, part, oth, vec, c1, c2, d1, d2, resid, low, low_t, grad, grad_t, buf):
    r = x[...].astype(f32) + part[...] + oth[...].astype(f32) + vec[4:5, :]
    resid[...] = r
    v = norm(r, vec[5:6, :], vec[6:7, :])[2].astype(bf16)
    low[...] = v
    low_t[...] = v.T
    assemble(scal, c1, c2, d1, d2, buf)
    g = jnp.where(kept_rows(scal), buf[...], 0.0).astype(bf16)
    grad[...] = g
    grad_t[...] = g.T


def gelu_both(v):
    half = 0.5 * (1.0 + lax.erf(v * 0.7071067811865476))
    slope = half + v * jnp.exp(-0.5 * v * v) * 0.3989422804014327
    return v * half, slope


def ffn_kernel(parts, first, last, split, adds):
    n = len({r for r, _ in parts})

    def kernel(scal, *refs):
        refs = list(refs)
        low, low_t, grad, grad_t = refs[:4]
        pieces, refs = refs[4 : 4 + n], refs[4 + n :]
        add_in = add_out = None
        if adds == "in":
            add_in = refs.pop(0)
        if adds == "out":
            add_out = refs.pop(0)
        if not first:
            old_out, old_back = refs.pop(0), refs.pop(0)
        if last:
            keep, give, back, back_low = refs[:4]
            refs = refs[4:]
        else:
            out, back = refs[:2]
            refs = refs[2:]
        if split:
            g_in, g_out = refs[0], refs[1]
            at = 0
            refs = refs[2:]
        else:
            g_in = g_out = refs[0]
            at = D + 16
            refs = refs[1:]
        ein, cout = refs
        z = scal[2]
        for s, (r, i) in enumerate(parts):
            src = pieces[r] if i is None else pieces[r].at[i]
            place = pl.ds(pl.multiple_of(((z - s + 4) % 4) * FEAT, FEAT), FEAT)
            ein[place, :] = src[0:FEAT, :]
            cout[place, :] = src[FEAT:WIDE, :]
            if s == 0:
                bias = src[WIDE:FPIECE, :].astype(f32)[0:1]
        act, slope = gelu_both(dot(low[...], ein[...]) + bias)
        hidden = act.astype(bf16)
        g = (dot(grad[...], cout[...]) * slope).astype(bf16)
        res = dot(hidden, cout[...], 1, 1)
        if not first:
            res = res + old_out[...]
        if last:
            core = scal[0] == 0
            a, b = res[:, :WIDE], res[:, WIDE:]
            keep[...] = jnp.where(core, a, b)
            give[...] = jnp.where(core, b, a).astype(bf16)
        else:
            out[...] = res
        res = dot(g, ein[...], 1, 1)
        if not first:
            res = res + old_back[...]
        back[...] = res
        if last:
            back_low[...] = res.astype(bf16)
        w = dot(low_t[...], g)
        sums = jnp.sum(g.astype(f32), 0, keepdims=True)
        sums = jnp.broadcast_to(sums, (16, WIDE))
        if add_in is not None:
            w = w + add_in[0:D, :].astype(f32)
            sums = sums + add_in[D : D + 16, :].astype(f32)
        g_in[0:D, :] = w.astype(bf16)
        g_in[D : D + 16, :] = sums.astype(bf16)
        w = dot(grad_t[...], hidden)
        if add_out is not None:
            w = w + add_out[...].astype(f32)
        g_out[at : at + D, :] = w.astype(bf16)

    return kernel


def ffn(scal, rows, pieces, parts, acc, split=False, last=False, add_in=None, add_out=None):
    first = acc is None
    adds = "in" if add_in is not None else "out" if add_out is not None else None
    extra = [a for a in (add_in, add_out) if a is not None]
    if last:
        outs = [((ROWS, WIDE), f32), ((ROWS, WIDE), bf16), ((ROWS, D), f32), ((ROWS, D), bf16)]
    else:
        outs = [((ROWS, D), f32), ((ROWS, D), f32)]
    if split:
        outs += [((D + 16, WIDE), bf16), ((D, WIDE), bf16)]
    else:
        outs += [((2 * D + 16, WIDE), bf16)]
    return call(ffn_kernel(parts, first, last, split, adds), outs, scal, *rows, *pieces, *extra, *(acc or ()),
                flops=12 * ROWS * D * WIDE, scratch=[pltpu.VMEM((D, WIDE), bf16)] * 2, name="ffn")


def place_rows(scal, v, out1, out2):
    even = scal[2] % 2 == 0
    q = []
    for i in range(2):
        part = v[:, i * FEAT : (i + 1) * FEAT]
        q.append(jnp.concatenate([part[0:HALF], part[PAD : PAD + HALF]], 1))
    out1[...] = jnp.where(even, q[0], q[1]).astype(bf16)
    out2[...] = jnp.where(even, q[1], q[0]).astype(bf16)


def k_out(scal, resid, keep, got, vec, out1, out2):
    first = scal[0] == 0
    r = jnp.where(first, resid[:, 0:WIDE], resid[:, WIDE:D])
    b = jnp.where(first, vec[7:8, 0:WIDE], vec[7:8, WIDE:D])
    v = r + keep[...] + got[...].astype(f32) + b
    place_rows(scal, jnp.where(kept_rows(scal), v, 0.0), out1, out2)


def k_back(scal, resid, back, back_oth, gml, vec, w, q, k, v, lse, mixed,
           gres, branch, gqk, gv, part, part_low, vrows, bufs, gmt, kt, qt, dqt, dk, dv):
    gnm = back[...] + back_oth[...].astype(f32)
    normed, inverse, _ = norm(resid[...], vec[5:6, :], vec[6:7, :])
    g = gml[...].astype(f32)
    res = g + norm_back(gnm, normed, inverse, vec[5:6, :])
    gres[...] = res
    low = res.astype(bf16)
    branch[...] = low
    vrows[...] = jnp.zeros_like(vrows)
    vrows[4:5, :] = jnp.sum(low.astype(f32), 0, keepdims=True)
    vrows[5:6, :] = jnp.sum(gnm * normed, 0, keepdims=True)
    vrows[6:7, :] = jnp.sum(gnm, 0, keepdims=True)
    vrows[7:8, :] = jnp.sum(g, 0, keepdims=True)
    keep = kept_rows(scal)
    lane = lax.broadcasted_iota(jnp.int32, (1, FEAT), 1) // HEAD_DIM
    none = jnp.zeros((), bf16)
    total = 0.0
    for j in range(2):
        gm = dot(low, w[j, 1, :, FEAT:WIDE])
        gm_low = gm.astype(bf16)
        gmt[...] = gm_low.T
        kt[...] = k[j].T
        qt[...] = q[j].T
        prod = gm_low.astype(f32) * mixed[j].astype(f32)
        prod_t = prod.T
        dk[...] = jnp.zeros_like(dk)
        dv[...] = jnp.zeros_like(dv)
        for h in range(3):
            rows = slice(h * HEAD_DIM, (h + 1) * HEAD_DIM)
            delta = jnp.sum(prod_t[rows, :], 0, keepdims=True)
            logits = jnp.where(keep, dot(jnp.where(lane == h, k[j], none), qt[...]), -1e30)
            chance = jnp.exp(logits - lse[3 * j + h : 3 * j + h + 1, :])
            gchance = dot(jnp.where(lane == h, v[j], none), gmt[...])
            gl = (chance * (gchance - delta)).astype(bf16)
            dv[...] += dot(chance.astype(bf16), jnp.where(lane == h, gm_low, none))
            dk[...] += dot(gl, jnp.where(lane == h, q[j], none))
            dqt[rows, :] = dot(kt[rows, :], gl) * 0.125
        gq = dqt[...].T
        both = jnp.concatenate([gq, dk[...]], 1).astype(bf16)
        gqk[j] = both
        val = dv[...].astype(bf16)
        gv[j] = val
        total += dot(both, w[j, 0], 1, 1) + dot(val, w[j, 1, :, 0:FEAT], 1, 1)
    part[...] = total
    part_low[...] = total.astype(bf16)


def k_front(scal, part, oth, x, vec, gres, branch, gqk, gv, mixed, ain_t, vrows,
            own, gx, gy, gd1, gd2, in1, in2, vfull, wbuf):
    core, hid, z = scal[0], scal[1], scal[2]
    gna = part[...] + oth[...].astype(f32)
    normed, inverse, _ = norm(x[...].astype(f32), vec[0:1, :], vec[1:2, :])
    res = gres[...] + norm_back(gna, normed, inverse, vec[0:1, :])
    place_rows(scal, jnp.where(core == 0, res[:, 0:WIDE], res[:, WIDE:D]), in1, in2)
    vfull[...] = vrows[...]
    vfull[0:1, :] = jnp.sum(gna * normed, 0, keepdims=True)
    vfull[1:2, :] = jnp.sum(gna, 0, keepdims=True)
    branch_t = branch[...].T
    dest = lambda i, p, j: ((own, gx, gy)[i].at[2 * p + j] if i < 3 else (gd1, gd2)[p].at[j])
    for j in range(2):
        wbuf[0] = dot(ain_t[...], gqk[j]).astype(bf16)
        wbuf[1, :, 0:FEAT] = dot(ain_t[...], gv[j]).astype(bf16)
        wbuf[1, :, FEAT:WIDE] = dot(branch_t, mixed[j]).astype(bf16)
        src = (z - 2 * core - j + 8) % 4
        mine = vfull[:, 0:FEAT]
        for i in (1, 2, 3):
            mine = jnp.where(src == i, vfull[:, i * FEAT : (i + 1) * FEAT], mine)
        line = lax.broadcasted_iota(jnp.int32, (8, 1), 0)
        cols_q = jnp.sum(gqk[j].astype(f32), 0, keepdims=True)[:, 0:FEAT]
        cols_v = jnp.sum(gv[j].astype(f32), 0, keepdims=True)
        mine = jnp.where(line == 2, cols_q, jnp.where(line == 3, cols_v, mine))
        mine = jnp.concatenate([mine, jnp.zeros_like(mine)], 1)
        mine = jnp.concatenate([mine, jnp.zeros_like(mine)], 0).astype(bf16)
        for i in range(4):
            for p in range(2):
                at = pl.multiple_of((4 * (core ^ p) + (hid ^ i)) * UNITS, 32)
                to = dest(i, p, j)
                to[0:UNITS, :] = wbuf[0, pl.ds(at, UNITS), :]
                to[UNITS : 2 * UNITS, :] = wbuf[1, pl.ds(at, UNITS), :]
                to[2 * UNITS : APIECE, :] = mine


def plus(a, b):
    return a.astype(f32) + b.astype(f32)


def k_fsum(scal, g, sx, sy, keep, s1, s2, s3):
    z = scal[2]
    for k, to in enumerate((keep, s1, s2, s3)):
        for base, at, n in ((((z + k) % 4) * FEAT, 0, FEAT), (D + 16 + ((z + k) % 4) * FEAT, FEAT, FEAT), (D, WIDE, 16)):
            rows = pl.ds(pl.multiple_of(base, 16), n)
            v = plus(g[rows, :], sx[rows, :]) + sy[rows, :].astype(f32)
            to[at : at + n, :] = v.astype(to.dtype)


def k_ffin(keep, r1, r2, r3, ex, con, bias):
    v = keep[...] + r1[...].astype(f32) + r2[...].astype(f32) + r3[...].astype(f32)
    ex[...] = v[0:FEAT]
    con[...] = v[FEAT:WIDE].T
    bias[...] = v[WIDE : WIDE + 1]


def k_aadd(gx, ry, gy, rx, px, py):
    px[0:2] = gx[0:2]
    px[2:4] = plus(gx[2:4], ry[...]).astype(bf16)
    py[0:2] = plus(gy[0:2], rx[...]).astype(bf16)
    py[2:4] = gy[2:4]


def k_asum(own, sx, sy, keep, give):
    keep[...] = plus(own[0:2], sx[0:2]) + sy[0:2].astype(f32)
    give[...] = (plus(own[2:4], sx[2:4]) + sy[2:4].astype(f32)).astype(bf16)


def k_asel(scal, keep, got, s0, s1, s2, s3):
    first = scal[0] == 0
    a, b = keep[...], got[...].astype(f32)
    lo, hi = jnp.where(first, a, b), jnp.where(first, b, a)
    s0[...] = lo[0]
    s1[...] = lo[1].astype(bf16)
    s2[...] = hi[0].astype(bf16)
    s3[...] = hi[1].astype(bf16)


def k_afin(s0, r1, r2, r3, pin, pout, vec):
    v = s0[...] + r1[...].astype(f32) + r2[...].astype(f32) + r3[...].astype(f32)
    pin[0] = v[0:UNITS, 0:FEAT]
    pin[1] = v[0:UNITS, FEAT:WIDE]
    pin[2] = v[UNITS : 2 * UNITS, 0:FEAT]
    pout[...] = v[UNITS : 2 * UNITS, FEAT:WIDE].T
    vec[...] = v[2 * UNITS : 2 * UNITS + 8, 0:FEAT]


def k_home(scal, b1, b2, out):
    even = scal[2] % 2 == 0
    a, b = b1[...], b2[...]
    s0, s1 = jnp.where(even, a, b), jnp.where(even, b, a)
    t = out.dtype
    out[0 : HALF - 1, 0, :] = s0[0 : HALF - 1].astype(t)
    left = lax.broadcasted_iota(jnp.int32, (1, WIDE), 1) < FEAT
    out[HALF - 1 : HALF, 0, :] = jnp.where(left, s0[HALF - 1 : HALF].astype(f32), s1[0:1].astype(f32)).astype(t)
    out[HALF:L, 0, :] = s1[1:HALF].astype(t)


def body(patches, visible, project_in, project_out, expand, contract, expand_bias, vectors, cotangent):
    n_dp = lax.axis_size("dp")
    more = n_dp // 2
    dp, hid, z = lax.axis_index("dp"), lax.axis_index("hid"), lax.axis_index("mod")
    core = dp % 2
    place = 4 * core + hid
    if more > 1:
        def mine_of(v, dim):
            whole = lax.all_gather(v, ("dp", "hid"), axis=dim, tiled=True)
            size = whole.shape[dim] // 8
            return lax.dynamic_slice_in_dim(whole, place * size, size, dim)

        project_in, project_out = mine_of(project_in, 1), mine_of(project_out, 1)
        expand, contract = mine_of(expand, 1), mine_of(contract, 0)
        expand_bias = mine_of(expand_bias, 0)

    counts = jnp.stack([visible, over_core(visible)])
    counts = jnp.where(core == 0, counts, counts[::-1]).reshape(4)
    scal = jnp.stack([core, hid, z, counts[z]]).astype(jnp.int32)
    where = jnp.stack([core, hid, z, z]).astype(jnp.int32)

    a0, f0 = call(k_pack, [((APIECE, WIDE), bf16), ((FPIECE, WIDE), bf16)], None,
                  project_in, project_out, expand, contract, expand_bias.reshape(1, -1), vectors, name="pack")
    a = [a0] + [over_z(a0, k) for k in (1, 2, 3)]
    block = ((HALF, WIDE), bf16)
    p1, p2, c1, c2 = call(k_in, [block] * 4, where, patches.reshape(L, 1, WIDE), cotangent.reshape(L, 1, WIDE), name="rows_in")
    p1, p2 = rows_there(p1, False), rows_there(p2, True)
    keeps, gives = call(k_give, [((2, 2 * UNITS, WIDE), bf16)] * 2, where, *a, name="give")
    got = over_core(gives)
    here = jnp.concatenate([keeps, got], 0)
    from_x, from_y = over_x(here), over_y(here)
    f = [f0] + [over_z(f0, k) for k in (1, 2, 3)]
    fx, fy = over_x(f0), over_y(f0)
    q1, q2 = over_core(p1), over_core(p2)
    diag_a, diag_b = over_x(from_y[:2]), over_y(from_x[2:])
    c1, c2 = rows_there(c1, False), rows_there(c2, True)
    d1, d2 = over_core(c1), over_core(c2)
    f3 = jnp.stack(f[1:])
    fx3, fy3 = over_x(f3), over_y(f3)
    fd_a, fd_b = over_x(jnp.stack([fy, fy3[0]])), over_y(fx3[1:])

    wide, tall = ((ROWS, D), bf16), ((D, ROWS), bf16)
    rows32 = ((ROWS, D), f32)
    x, ain, ain_t, vec, slots = call(
        k_norm1, [wide, wide, tall, ((8, D), f32), ((2, 8, FEAT), f32)], scal, p1, p2, q1, q2, *a,
        scratch=[pltpu.VMEM((ROWS, D), f32)], name="norm_attn")
    head = ((2, ROWS, FEAT), bf16)
    flip = pltpu.VMEM((2, FEAT, ROWS), bf16)
    w, q, k, v, lse, mixed, part, part_low = call(
        k_attn, [((2, 2, D, WIDE), bf16), head, head, head, ((8, ROWS), f32), head, rows32, wide], scal,
        ain, keeps, got, from_x, from_y, diag_a, diag_b, slots,
        flops=2 * ROWS * D * WIDE * 4 + 24 * ROWS * ROWS * HEAD_DIM,
        scratch=[flip, flip, pltpu.VMEM((2, FEAT, ROWS), f32)], name="attend")
    other = over_core(part_low)
    resid, low, low_t, gml, gml_t = call(
        k_norm2, [rows32, wide, tall, wide, tall], scal, x, part, other, vec, c1, c2, d1, d2,
        scratch=[pltpu.VMEM((ROWS, D), f32)], name="norm_mlp")

    rows = (low, low_t, gml, gml_t)
    o_acc, b_acc, g_own = ffn(scal, rows, f, [(i, None) for i in range(4)], None)
    o_acc, b_acc, gd_in, gd_out = ffn(scal, rows, (fd_a, fd_b), [(0, 0), (0, 1), (1, 0), (1, 1)], (o_acc, b_acc), split=True)
    rx, ry = over_x(gd_in), over_y(gd_out)
    one_three = [(0, None), (1, 0), (1, 1), (1, 2)]
    o_acc, b_acc, g_x = ffn(scal, rows, (fx, fx3), one_three, (o_acc, b_acc), add_out=ry)
    sx = over_x(g_x)
    keep, give, back, back_low, g_y = ffn(scal, rows, (fy, fy3), one_three, (o_acc, b_acc), last=True, add_in=rx)
    back_oth = over_core(back_low)
    sy = over_y(g_y)
    got_out = over_core(give)
    r1, r2 = call(k_out, [block] * 2, scal, resid, keep, got_out, vec, name="result")

    pair = ((2, ROWS, WIDE), bf16)
    side = pltpu.VMEM((FEAT, ROWS), bf16)
    acc = pltpu.VMEM((ROWS, FEAT), f32)
    gres, branch, gqk, gv, part, part_low, vrows = call(
        k_back, [rows32, wide, pair, head, rows32, wide, ((8, D), f32)], scal,
        resid, back, back_oth, gml, vec, w, q, k, v, lse, mixed,
        flops=2 * ROWS * D * WIDE * 4 + 60 * ROWS * ROWS * HEAD_DIM,
        scratch=[pltpu.VMEM((8, ROWS), f32), side, side, side, pltpu.VMEM((FEAT, ROWS), f32), acc, acc], name="attend_back")
    oth = over_core(part_low)
    r1, r2 = rows_back(r1, False), rows_back(r2, True)
    four, two = ((4, APIECE, WIDE), bf16), ((2, APIECE, WIDE), bf16)
    ga_own, ga_x, ga_y, ga_d1, ga_d2, i1, i2 = call(
        k_front, [four, four, four, two, two, block, block], where, part, oth, x, vec, gres, branch, gqk, gv, mixed, ain_t, vrows,
        flops=2 * ROWS * D * WIDE * 4, scratch=[pltpu.VMEM((8, D), f32), pltpu.VMEM((2, D, WIDE), bf16)], name="norm_attn_back")
    ax, ay = over_x(ga_d1), over_y(ga_d2)
    fpart = (FPIECE, WIDE)
    fk, f1, f2, f3 = call(k_fsum, [(fpart, f32)] + [(fpart, bf16)] * 3, where, g_own, sx, sy, name="ffn_sum")
    px, py = call(k_aadd, [four, four], None, ga_x, ay, ga_y, ax, name="attn_add")
    tx, ty = over_x(px), over_y(py)
    f1, f2, f3 = over_z(f1, 1), over_z(f2, 2), over_z(f3, 3)
    i1, i2 = rows_back(i1, False), rows_back(i2, True)
    result = call(k_home, [((L, 1, WIDE), bf16)], where, r1, r2, name="rows_out").reshape(1, L * WIDE)
    expand_grad, contract_grad, bias_grad = call(
        k_ffin, [((FEAT, WIDE), f32), ((WIDE, FEAT), f32), ((1, WIDE), f32)], None, fk, f1, f2, f3, name="ffn_last")
    apart = (APIECE, WIDE)
    ak, give = call(k_asum, [((2,) + apart, f32), ((2,) + apart, bf16)], None, ga_own, tx, ty, name="attn_sum")
    got = over_core(give)
    s0, s1, s2, s3 = call(k_asel, [(apart, f32)] + [(apart, bf16)] * 3, where, ak, got, name="attn_slots")
    s1, s2, s3 = over_z(s1, 3), over_z(s2, 2), over_z(s3, 1)
    grad_input = call(k_home, [((L, 1, WIDE), f32)], where, i1, i2, name="rows_out_grad").reshape(1, L * WIDE)
    in_grad, out_grad, vector_grad = call(
        k_afin, [((3, UNITS, FEAT), f32), ((FEAT, UNITS), f32), ((8, FEAT), f32)], None, s0, s1, s2, s3, name="attn_last")
    bias_grad = bias_grad.reshape(-1)

    if more > 1:
        def spread(v, dim):
            whole = jnp.zeros(v.shape[:dim] + (8 * v.shape[dim],) + v.shape[dim + 1 :], f32)
            whole = lax.dynamic_update_slice_in_dim(whole, v, place * v.shape[dim], dim)
            return lax.psum_scatter(whole, ("dp", "hid"), scatter_dimension=dim, tiled=True)

        in_grad, out_grad = spread(in_grad, 1), spread(out_grad, 1)
        expand_grad, contract_grad, bias_grad = spread(expand_grad, 1), spread(contract_grad, 0), spread(bias_grad, 0)
        vector_grad = lax.psum(vector_grad, "dp") / 2
    return result, grad_input, in_grad, out_grad, expand_grad, contract_grad, bias_grad, vector_grad


def solution(mesh):
    rows = P("mod", ("dp", "hid"))
    in_specs = (rows, P(("dp", "hid")), P(None, ("dp", "hid"), "mod"), rows, rows, P(("dp", "hid"), "mod"),
                P(("dp", "hid")), P(None, "mod"), rows)
    out_specs = (rows, rows, P(None, ("dp", "hid"), "mod"), rows, rows, P(("dp", "hid"), "mod"),
                 P(("dp", "hid")), P(None, "mod"))
    return jax.shard_map(body, mesh=mesh, in_specs=in_specs, out_specs=out_specs, check_vma=False)
```

time: 397 us -> 311 us (0.78)
  waiting for transfers between devices: 47.3 us -> 154 us
  other arithmetic: 107 us -> 3.74 us
  Pallas kernels: 0 us -> 71.7 us
  matrix products: 62.1 us -> 0 us
  local copies, waits for them, and re-layouts: 58.8 us -> 10.6 us
  starting transfers between devices: 111 us -> 65 us
    pallas_call x0 -> x21, Pallas kernels: none -> 71.7 us  [call(): pl.pallas_call(kernel, out_shape=outs[0] if single else outs, in_specs=in...]
    dot_general x78 -> x0, matrix products: 62.1 us -> none  [dot(): lax.dot_general(a, b, (((ca,), (cb,)), ((), ())), preferred_element_type=...]
    ppermute x9, waiting for transfers between devices: 6.35 us -> 44.4 us  [over_x(): return lax.ppermute(v, 'hid', X)]
    ppermute x8 -> x11, starting transfers between devices: 41.1 us -> 9.67 us  [over_core(): return lax.ppermute(v, 'dp', [(i, i ^ 1) for i in range(n)])]
    select_n x13 -> x0, other arithmetic: 27.7 us -> none  [the longest x1 17.3 us: unflat(): jnp.where(core == 0, own[1], oth[1])]
    ppermute x12, waiting for transfers between devices: 18.2 us -> 44.3 us  [over_z(): return lax.ppermute(v, 'mod', [(i, (i + shift) % n) for i in range(n)])]
    concatenate x19 -> x0, other arithmetic: 21.5 us -> none  [the longest x1 7.54 us: home(): return jnp.concatenate([s0[:, :edge], s1[:, FEAT:]], 1)]
    convert_element_type x27 -> x0, other arithmetic: 21.1 us -> none  [the longest x2 7.68 us: body(): grad_input = home(grad_in.astype(bf16)).astype(f32)]
  transfers between devices with their start and end apart: 44 -> 49, of which waited for: 7 -> 20; matrix products, arithmetic and copies ran while one was open for 47% -> 2% of each run, Pallas kernels for 0% -> 14%
where the time goes in v2:
time: 311 us; the launch traced here: 307 us
  waiting for transfers between devices  154 us (50%)
  Pallas kernels  71.7 us (23%)
  starting transfers between devices  65 us (21%)
  local copies, waits for them, and re-layouts  10.6 us (3%)
  other arithmetic  3.74 us (1%)
    pallas_call x21, Pallas kernels, call(): pl.pallas_call(kernel, out_shape=outs[0] if single else outs, in_specs=in...  71.7 us
    ppermute x9, waiting for transfers between devices, over_x(): return lax.ppermute(v, 'hid', X)  44.4 us
    ppermute x12, waiting for transfers between devices, over_z(): return lax.ppermute(v, 'mod', [(i, (i + shift) % n) for i in range(n)])  44.3 us
    ppermute x12, starting transfers between devices, over_z(): return lax.ppermute(v, 'mod', [(i, (i + shift) % n) for i in range(n)])  29.8 us
    ppermute x9, waiting for transfers between devices, over_y(): return lax.ppermute(v, 'hid', Y)  29.3 us
    ppermute x4, waiting for transfers between devices, rows_back(): return lax.ppermute(v, ('dp', 'mod'), row_pairs(second, True))  22.4 us
    ppermute x9, starting transfers between devices, over_x(): return lax.ppermute(v, 'hid', X)  10.4 us
    ppermute x11, waiting for transfers between devices, over_core(): return lax.ppermute(v, 'dp', [(i, i ^ 1) for i in range(n)])  9.92 us
  transfers between devices with their start and end apart: 49, of which 20 were waited for; matrix products, arithmetic and copies ran while one was open for 2% of the time, Pallas kernels for 14%

profile of v2, /device:TPU:0, one launch (start us, length us, event | category | flops | bytes accessed | tf_op | source)
XLA Modules:
  0.0 306.5 jit_solution(5269631326981330104)
XLA Ops:
  6.1 5.1 %collective-permute-start.7 = (bf16[208,384]{1,0:T(8,128)(2,1)S(1)}, bf16[208,384]{1,0:T(8,128)(2,1)S(1)}, u32[]{:S(2)}, u32[]{:S(2)}) collective-permute-start(bf16[208,384]{1,0:T(8,128)(2,1)S(1)} %get-tuple-element.85.a0), channel_id=1, source_target_pairs={{0,3},{1,0},{2,1},{3,2},{4,7},{5,4},{6,5},{7,6},{8,11},{9,8},{10,9... | collective-permute-start | bytes 479240 | tf_op jit(solution)/shard_map/ppermute | solution.py:46
  16.3 8.4 %collective-permute-done.6.a2 = bf16[208,384]{1,0:T(8,128)(2,1)S(1)} collective-permute-done((bf16[208,384]{1,0:T(8,128)(2,1)S(1)}, bf16[208,384]{1,0:T(8,128)(2,1)S(1)}, u32[]{:S(2)}, u32[]{:S(2)}) %collective-permute-start.6) | collective-permute-done | bytes 159776 | tf_op jit(solution)/shard_map/ppermute | solution.py:46
  29.8 1.6 collective-permute-start.20
  31.4 2.0 collective-permute-start.19
  34.9 2.4 rows_in.1
  38.5 22.2 %collective-permute-done.20.refs_6_ = bf16[400,384]{1,0:T(8,128)(2,1)S(1)} collective-permute-done((bf16[400,384]{1,0:T(8,128)(2,1)S(1)}, bf16[400,384]{1,0:T(8,128)(2,1)S(1)}, u32[]{:S(2)}, u32[]{:S(2)}) %collective-permute-start.20) | collective-permute-done | bytes 307232 | tf_op jit(solution)/shard_map/ppermute | solution.py:46
  64.6 4.1 %collective-permute-done.2.own2 = bf16[265,384]{1,0:T(8,128)(2,1)S(1)} collective-permute-done((bf16[265,384]{1,0:T(8,128)(2,1)S(1)}, bf16[265,384]{1,0:T(8,128)(2,1)S(1)}, u32[]{:S(2)}, u32[]{:S(2)}) %collective-permute-start.2) | collective-permute-done | bytes 203552 | tf_op jit(solution)/shard_map/ppermute | solution.py:61
  72.2 1.7 norm_attn.1
  75.8 13.1 %collective-permute-done.11.da = bf16[2,192,384]{2,1,0:T(8,128)(2,1)S(1)} collective-permute-done((bf16[2,192,384]{2,1,0:T(8,128)(2,1)S(1)}, bf16[2,192,384]{2,1,0:T(8,128)(2,1)S(1)}, u32[]{:S(2)}, u32[]{:S(2)}) %collective-permute-start.11) | collective-permute-done | bytes 294944 | tf_op jit(solution)/shard_map/ppermute | solution.py:32
  88.8 3.1 %collective-permute-done.12.db = bf16[2,192,384]{2,1,0:T(8,128)(2,1)S(1)} collective-permute-done((bf16[2,192,384]{2,1,0:T(8,128)(2,1)S(1)}, bf16[2,192,384]{2,1,0:T(8,128)(2,1)S(1)}, u32[]{:S(2)}, u32[]{:S(2)}) %collective-permute-start.12) | collective-permute-done | bytes 294944 | tf_op jit(solution)/shard_map/ppermute | solution.py:36
  92.0 9.2 %attend.1 = (bf16[2,2,768,384]{3,2,1,0:T(8,128)(2,1)}, bf16[2,544,192]{2,1,0:T(8,128)(2,1)S(1)}, bf16[2,544,192]{2,1,0:T(8,128)(2,1)S(1)}, bf16[2,544,192]{2,1,0...) custom-call(s32[4]{0:T(128)S(1)} %get-tuple-element.166.scal, ...), custom_call_target="tpu_custom_call" | custom-call | flops 1738014720 | bytes 9761792 | tf_op jit(solution)/shard_map/attend/pallas_call | solution.py:79
  104.5 1.8 collective-permute-start.15
  106.3 9.3 %collective-permute-start.16 = (bf16[265,384]{1,0:T(8,128)(2,1)S(1)}, bf16[265,384]{1,0:T(8,128)(2,1)S(1)}, u32[]{:S(2)}, u32[]{:S(2)}) collective-permute-start(bf16[265,384]{1,0:T(8,128)(2,1)S(1)} %collective-permute-done.14.c1), channel_id=1, source_target_pairs={{0,16},{16,0},{1,17},{17,1},{2,18},{18,2},{3,19},{19,3},{4,20},{20... | collective-permute-start | bytes 610568 | tf_op jit(solution)/shard_map/ppermute | solution.py:41
  117.1 3.7 %norm_mlp.1 = (f32[544,768]{1,0:T(8,128)}, bf16[544,768]{1,0:T(8,128)(2,1)S(1)}, bf16[768,544]{1,0:T(8,128)(2,1)S(1)}, bf16[544,768]{1,0:T(8,128)(2,1)S(1)}, bf16[768,544]{1,0:T(8,128)(2,1)S(1)}) custom-call(s32[4]{0:T(128)S(1)} %get-tuple-element.166.scal, bf16[544,768]{1,0:T(8,128)(2,1)S(1)} %get-tuple-element.86.x, f32[544,768]{1,0:T(8,128)} %get-tuple-element.91.part, ...), custom_call_target="tpu_custom_call" | custom-call | bytes 9194496 | tf_op jit(solution)/shard_map/norm_mlp/pallas_call | solution.py:79
  120.8 5.4 %ffn.4 = (f32[544,768]{1,0:T(8,128)}, f32[544,768]{1,0:T(8,128)}, bf16[1552,384]{1,0:T(8,128)(2,1)S(1)}) custom-call(s32[4]{0:T(128)S(1)} %get-tuple-element.166.scal, bf16[544,768]{1,0:T(8,128)(2,1)S(1)} %get-tuple-element.97.refs_0_, bf16[768,544]{1,0:T(8,128)(2,1)S(1)} %get-tuple-element.98.refs_1_, bf16[544,768]{1,0:T(8,128)(2,1)S(1)} %get-tuple-element.99.refs_2_.gml, ...), custom_call_target="tpu_custom_call" | custom-call | flops 1925185536 | bytes 9105408 | tf_op jit(solution)/shard_map/ffn/pallas_call | solution.py:79
  126.2 5.9 %ffn.5 = (f32[544,768]{1,0:T(8,128)}, f32[544,768]{1,0:T(8,128)}, bf16[784,384]{1,0:T(8,128)(2,1)S(1)}, bf16[768,384]{1,0:T(8,128)(2,1)S(1)}) custom-call(s32[4]{0:T(128)S(1)} %get-tuple-element.166.scal, bf16[544,768]{1,0:T(8,128)(2,1)S(1)} %get-tuple-element.97.refs_0_, bf16[768,544]{1,0:T(8,128)(2,1)S(1)} %get-tuple-element.98.refs_1_, ...), custom_call_target="tpu_custom_call" | custom-call | flops 1925185536 | bytes 12447744 | tf_op jit(solution)/shard_map/ffn/pallas_call | solution.py:79
  135.6 20.0 %collective-permute-done.27.refs_4_ = bf16[400,384]{1,0:T(8,128)(2,1)S(1)} collective-permute-done((bf16[400,384]{1,0:T(8,128)(2,1)S(1)}, bf16[400,384]{1,0:T(8,128)(2,1)S(1)}, u32[]{:S(2)}, u32[]{:S(2)}) %collective-permute-start.27) | collective-permute-done | bytes 307232 | tf_op jit(solution)/shard_map/ppermute | solution.py:32
  155.7 6.2 %ffn.6 = (f32[544,768]{1,0:T(8,128)}, f32[544,768]{1,0:T(8,128)}, bf16[1552,384]{1,0:T(8,128)(2,1)}) custom-call(s32[4]{0:T(128)S(1)} %get-tuple-element.166.scal, bf16[544,768]{1,0:T(8,128)(2,1)S(1)} %get-tuple-element.97.refs_0_, bf16[768,544]{1,0:T(8,128)(2,1)S(1)} %get-tuple-element.98.refs_1_, bf16[544,768]{1,0:T(8,128)(2,1)S(1)} %get-tuple-element.99.refs_2_.gml, ...), custom_call_target="tpu_custom_call" | custom-call | flops 1925185536 | bytes 13037568 | tf_op jit(solution)/shard_map/ffn/pallas_call | solution.py:79
  161.9 7.2 %ffn.7 = (f32[544,384]{1,0:T(8,128)S(1)}, bf16[544,384]{1,0:T(8,128)(2,1)S(1)}, f32[544,768]{1,0:T(8,128)}, bf16[544,768]{1,0:T(8,128)(2,1)S(1)}, bf16[1552,384]{1,0:T(8,128)(2,1)}) custom-call(s32[4]{0:T(128)S(1)} %get-tuple-element.166.scal, bf16[544,768]{1,0:T(8,128)(2,1)S(1)} %get-tuple-element.97.refs_0_, bf16[768,544]{1,0:T(8,128)(2,1)} %copy-done.1, ...), custom_call_target="tpu_custom_call" | custom-call | flops 1925185536 | bytes 13467648 | tf_op jit(solution)/shard_map/ffn/pallas_call | solution.py:79
  169.1 2.4 collective-permute-done.32.back_oth
  171.5 14.3 %attend_back.1 = (f32[544,768]{1,0:T(8,128)}, bf16[544,768]{1,0:T(8,128)(2,1)S(1)}, bf16[2,544,384]{2,1,0:T(8,128)(2,1)S(1)}, bf16[2,544,192]{2,1,0:T(8,128)(2,1...) custom-call(s32[4]{0:T(128)S(1)} %get-tuple-element.166.scal, ...), custom_call_target="tpu_custom_call" | custom-call | flops 2419851264 | bytes 15377408 | tf_op jit(solution)/shard_map/attend_back/pallas_call | solution.py:79
  189.9 6.7 %norm_attn_back.1 = (bf16[4,208,384]{2,1,0:T(8,128)(2,1)S(1)}, bf16[4,208,384]{2,1,0:T(8,128)(2,1)S(1)}, bf16[4,208,384]{2,1,0:T(8,128)(2,1)S(1)}, bf16[2,208,38...) custom-call(s32[4]{0:T(128)S(1)} %pad_add_fusion.1.scal, ...), custom_call_target="tpu_custom_call" | custom-call | flops 1283457024 | bytes 11367936 | tf_op jit(solution)/shard_map/norm_attn_back/pallas_call | solution.py:79
  198.8 25.8 %collective-permute-done.36.ry = bf16[2,208,384]{2,1,0:T(8,128)(2,1)S(1)} collective-permute-done((bf16[2,208,384]{2,1,0:T(8,128)(2,1)S(1)}, bf16[2,208,384]{2,1,0:T(8,128)(2,1)S(1)}, u32[]{:S(2)}, u32[]{:S(2)}) %collective-permute-start.36) | collective-permute-done | bytes 319520 | tf_op jit(solution)/shard_map/ppermute | solution.py:36
  225.8 1.8 collective-permute-done.29.got
  229.2 11.2 %collective-permute-done.38.sx = bf16[4,208,384]{2,1,0:T(8,128)(2,1)S(1)} collective-permute-done((bf16[4,208,384]{2,1,0:T(8,128)(2,1)S(1)}, bf16[4,208,384]{2,1,0:T(8,128)(2,1)S(1)}, u32[]{:S(2)}, u32[]{:S(2)}) %collective-permute-start.38) | collective-permute-done | bytes 639008 | tf_op jit(solution)/shard_map/ppermute | solution.py:32
  242.0 2.9 collective-permute-start.46
  245.5 2.8 collective-permute-start.48
  248.3 22.3 %collective-permute-done.31.b2 = bf16[265,384]{1,0:T(8,128)(2,1)S(1)} collective-permute-done((bf16[265,384]{1,0:T(8,128)(2,1)S(1)}, bf16[265,384]{1,0:T(8,128)(2,1)S(1)}, u32[]{:S(2)}, u32[]{:S(2)}) %collective-permute-start.31) | collective-permute-done | bytes 203552 | tf_op jit(solution)/shard_map/ppermute | solution.py:65
  273.7 11.9 %collective-permute-start.41 = (bf16[208,384]{1,0:T(8,128)(2,1)S(1)}, bf16[208,384]{1,0:T(8,128)(2,1)S(1)}, u32[]{:S(2)}, u32[]{:S(2)}) collective-permute-start(bf16[208,384]{1,0:T(8,128)(2,1)S(1)} %get-tuple-element.142), channel_id=1, source_target_pairs={{0,3},{1,0},{2,1},{3,2},{4,7},{5,4},{6,5},{7,6},{8,11},{9,8},{10,9... | collective-permute-start | bytes 479240 | tf_op jit(solution)/shard_map/ppermute | solution.py:46
  286.3 1.7 rows_out.1
  290.4 1.7 rows_out_grad.1
  292.0 13.4 %collective-permute-done.42.r2 = bf16[208,384]{1,0:T(8,128)(2,1)S(1)} collective-permute-done((bf16[208,384]{1,0:T(8,128)(2,1)S(1)}, bf16[208,384]{1,0:T(8,128)(2,1)S(1)}, u32[]{:S(2)}, u32[]{:S(2)}) %collective-permute-start.42) | collective-permute-done | bytes 159776 | tf_op jit(solution)/shard_map/ppermute | solution.py:46
  (134 shorter events, 54.1 us)
Async XLA Ops:
  27.0 35.9 %collective-permute-start.10 = (bf16[4,192,384]{2,1,0:T(8,128)(2,1)S(1)}, bf16[4,192,384]{2,1,0:T(8,128)(2,1)S(1)}, u32[]{:S(2)}, u32[]{:S(2)}) collective-permute-start(bf16[4,192,384]{2,1,0:T(8,128)(2,1)S(1)} %constant_dynamic-update-slice_fusion), channel_id=1, source_target_pairs={{0,8},{8,0},{4,12},{12,4},{1,9},{9,1},{5,13},{13,5},{2,10},{10,2},... | collective-permute-start | bytes 1769480 | tf_op jit(solution)/shard_map/ppermute | solution.py:36
  29.8 30.9 %collective-permute-start.20 = (bf16[400,384]{1,0:T(8,128)(2,1)S(1)}, bf16[400,384]{1,0:T(8,128)(2,1)S(1)}, u32[]{:S(2)}, u32[]{:S(2)}) collective-permute-start(bf16[400,384]{1,0:T(8,128)(2,1)S(1)} %get-tuple-element.101.refs_4_), channel_id=1, source_target_pairs={{0,2},{1,3},{2,0},{3,1},{4,6},{5,7},{6,4},{7,5},{8,10},{9,11},{10,... | collective-permute-start | bytes 921608 | tf_op jit(solution)/shard_map/ppermute | solution.py:46
  31.4 29.3 %collective-permute-start.19 = (bf16[400,384]{1,0:T(8,128)(2,1)S(1)}, bf16[400,384]{1,0:T(8,128)(2,1)S(1)}, u32[]{:S(2)}, u32[]{:S(2)}) collective-permute-start(bf16[400,384]{1,0:T(8,128)(2,1)S(1)} %get-tuple-element.101.refs_4_), channel_id=1, source_target_pairs={{0,1},{1,2},{2,3},{3,0},{4,5},{5,6},{6,7},{7,4},{8,9},{9,10},{10,1... | collective-permute-start | bytes 921608 | tf_op jit(solution)/shard_map/ppermute | solution.py:46
  33.4 29.6 %collective-permute-start.9 = (bf16[4,192,384]{2,1,0:T(8,128)(2,1)S(1)}, bf16[4,192,384]{2,1,0:T(8,128)(2,1)S(1)}, u32[]{:S(2)}, u32[]{:S(2)}) collective-permute-start(bf16[4,192,384]{2,1,0:T(8,128)(2,1)S(1)} %constant_dynamic-update-slice_fusion), channel_id=1, source_target_pairs={{0,4},{4,0},{8,12},{12,8},{1,5},{5,1},{9,13},{13,9},{2,6},{6,2},{1... | collective-permute-start | bytes 1769480 | tf_op jit(solution)/shard_map/ppermute | solution.py:32
  37.6 24.7 %collective-permute-start.1 = (bf16[265,384]{1,0:T(8,128)(2,1)S(1)}, bf16[265,384]{1,0:T(8,128)(2,1)S(1)}, u32[]{:S(2)}, u32[]{:S(2)}) collective-permute-start(bf16[265,384]{1,0:T(8,128)(2,1)S(1)} %get-tuple-element.83), channel_id=1, source_target_pairs={{0,0},{1,1},{2,16},{3,17},{16,2},{17,3},{18,18},{19,19},{4,4},{5,5... | collective-permute-start | bytes 610568 | tf_op jit(solution)/shard_map/ppermute | solution.py:61
  60.8 40.3 %collective-permute-start.24 = (bf16[3,400,384]{2,1,0:T(8,128)(2,1)S(1)}, bf16[3,400,384]{2,1,0:T(8,128)(2,1)S(1)}, u32[]{:S(2)}, u32[]{:S(2)}) collective-permute-start(bf16[3,400,384]{2,1,0:T(8,128)(2,1)S(1)} %pad_maximum_fusion), channel_id=1, source_target_pairs={{0,4},{4,0},{8,12},{12,8},{1,5},{5,1},{9,13},{13,9},{2,6},{6,2},{1... | collective-permute-start | bytes 2764808 | tf_op jit(solution)/shard_map/ppermute | solution.py:32
  62.4 39.4 %collective-permute-start.22 = (bf16[3,400,384]{2,1,0:T(8,128)(2,1)S(1)}, bf16[3,400,384]{2,1,0:T(8,128)(2,1)S(1)}, u32[]{:S(2)}, u32[]{:S(2)}) collective-permute-start(bf16[3,400,384]{2,1,0:T(8,128)(2,1)S(1)} %pad_maximum_fusion), channel_id=1, source_target_pairs={{0,8},{8,0},{4,12},{12,4},{1,9},{9,1},{5,13},{13,5},{2,10},{10,2},... | collective-permute-start | bytes 2764808 | tf_op jit(solution)/shard_map/ppermute | solution.py:36
  63.0 25.8 %collective-permute-start.11 = (bf16[2,192,384]{2,1,0:T(8,128)(2,1)S(1)}, bf16[2,192,384]{2,1,0:T(8,128)(2,1)S(1)}, u32[]{:S(2)}, u32[]{:S(2)}) collective-permute-start(bf16[2,192,384]{2,1,0:T(8,128)(2,1)S(1)} %slice.16), channel_id=1, source_target_pairs={{0,4},{4,0},{8,12},{12,8},{1,5},{5,1},{9,13},{13,9},{2,6},{6,2},{1... | collective-permute-start | bytes 884744 | tf_op jit(solution)/shard_map/ppermute | solution.py:32
  68.7 23.2 %collective-permute-start.12 = (bf16[2,192,384]{2,1,0:T(8,128)(2,1)S(1)}, bf16[2,192,384]{2,1,0:T(8,128)(2,1)S(1)}, u32[]{:S(2)}, u32[]{:S(2)}) collective-permute-start(bf16[2,192,384]{2,1,0:T(8,128)(2,1)S(1)} %slice.17), channel_id=1, source_target_pairs={{0,8},{8,0},{4,12},{12,4},{1,9},{9,1},{5,13},{13,5},{2,10},{10,2},... | collective-permute-start | bytes 884744 | tf_op jit(solution)/shard_map/ppermute | solution.py:36
  70.7 31.1 %collective-permute-start.18 = (bf16[400,384]{1,0:T(8,128)(2,1)S(1)}, bf16[400,384]{1,0:T(8,128)(2,1)S(1)}, u32[]{:S(2)}, u32[]{:S(2)}) collective-permute-start(bf16[400,384]{1,0:T(8,128)(2,1)S(1)} %get-tuple-element.101.refs_4_), channel_id=1, source_target_pairs={{0,8},{8,0},{4,12},{12,4},{1,9},{9,1},{5,13},{13,5},{2,10},{10,2},... | collective-permute-start | bytes 921608 | tf_op jit(solution)/shard_map/ppermute | solution.py:36
  101.1 16.0 %collective-permute-start.13 = (bf16[544,768]{1,0:T(8,128)(2,1)S(1)}, bf16[544,768]{1,0:T(8,128)(2,1)S(1)}, u32[]{:S(2)}, u32[]{:S(2)}) collective-permute-start(bf16[544,768]{1,0:T(8,128)(2,1)S(1)} %get-tuple-element.92), channel_id=1, source_target_pairs={{0,16},{16,0},{1,17},{17,1},{2,18},{18,2},{3,19},{19,3},{4,20},{20... | collective-permute-start | bytes 2506760 | tf_op jit(solution)/shard_map/ppermute | solution.py:41
  101.2 25.0 %collective-permute-start.25 = (bf16[2,400,384]{2,1,0:T(8,128)(2,1)S(1)}, bf16[2,400,384]{2,1,0:T(8,128)(2,1)S(1)}, u32[]{:S(2)}, u32[]{:S(2)}) collective-permute-start(bf16[2,400,384]{2,1,0:T(8,128)(2,1)S(1)} %slice.19), channel_id=1, source_target_pairs={{0,8},{8,0},{4,12},{12,4},{1,9},{9,1},{5,13},{13,5},{2,10},{10,2},... | collective-permute-start | bytes 1843208 | tf_op jit(solution)/shard_map/ppermute | solution.py:36
  102.7 23.5 %collective-permute-start.23 = (bf16[2,400,384]{2,1,0:T(8,128)(2,1)}, bf16[2,400,384]{2,1,0:T(8,128)(2,1)S(1)}, u32[]{:S(2)}, u32[]{:S(2)}) collective-permute-start(bf16[2,400,384]{2,1,0:T(8,128)(2,1)} %pad_maximum_fusion.1), channel_id=1, source_target_pairs={{0,4},{4,0},{8,12},{12,8},{1,5},{5,1},{9,13},{13,9},{2,6},{6,2},{1... | collective-permute-start | bytes 1843208 | tf_op jit(solution)/shard_map/ppermute | solution.py:32
  132.1 23.6 %collective-permute-start.28 = (bf16[768,384]{1,0:T(8,128)(2,1)S(1)}, bf16[768,384]{1,0:T(8,128)(2,1)S(1)}, u32[]{:S(2)}, u32[]{:S(2)}) collective-permute-start(bf16[768,384]{1,0:T(8,128)(2,1)S(1)} %get-tuple-element.105), channel_id=1, source_target_pairs={{0,8},{8,0},{4,12},{12,4},{1,9},{9,1},{5,13},{13,5},{2,10},{10,2},... | collective-permute-start | bytes 1769480 | tf_op jit(solution)/shard_map/ppermute | solution.py:36
  133.6 28.3 %collective-permute-start.26 = (bf16[784,384]{1,0:T(8,128)(2,1)S(1)}, bf16[784,384]{1,0:T(8,128)(2,1)S(1)}, u32[]{:S(2)}, u32[]{:S(2)}) collective-permute-start(bf16[784,384]{1,0:T(8,128)(2,1)S(1)} %get-tuple-element.104), channel_id=1, source_target_pairs={{0,4},{4,0},{8,12},{12,8},{1,5},{5,1},{9,13},{13,9},{2,6},{6,2},{1... | collective-permute-start | bytes 1806344 | tf_op jit(solution)/shard_map/ppermute | solution.py:32
  135.2 20.5 %collective-permute-start.27 = (bf16[400,384]{1,0:T(8,128)(2,1)S(1)}, bf16[400,384]{1,0:T(8,128)(2,1)S(1)}, u32[]{:S(2)}, u32[]{:S(2)}) collective-permute-start(bf16[400,384]{1,0:T(8,128)(2,1)S(1)} %get-tuple-element.101.refs_4_), channel_id=1, source_target_pairs={{0,4},{4,0},{8,12},{12,8},{1,5},{5,1},{9,13},{13,9},{2,6},{6,2},{1... | collective-permute-start | bytes 921608 | tf_op jit(solution)/shard_map/ppermute | solution.py:32
  187.7 53.3 %collective-permute-start.44 = (bf16[1552,384]{1,0:T(8,128)(2,1)}, bf16[1552,384]{1,0:T(8,128)(2,1)S(1)}, u32[]{:S(2)}, u32[]{:S(2)}) collective-permute-start(bf16[1552,384]{1,0:T(8,128)(2,1)} %get-tuple-element.148), channel_id=1, source_target_pairs={{0,4},{4,0},{8,12},{12,8},{1,5},{5,1},{9,13},{13,9},{2,6},{6,2},{1... | collective-permute-start | bytes 3575816 | tf_op jit(solution)/shard_map/ppermute | solution.py:32
  189.3 51.7 %collective-permute-start.45 = (bf16[1552,384]{1,0:T(8,128)(2,1)}, bf16[1552,384]{1,0:T(8,128)(2,1)S(1)}, u32[]{:S(2)}, u32[]{:S(2)}) collective-permute-start(bf16[1552,384]{1,0:T(8,128)(2,1)} %get-tuple-element.149), channel_id=1, source_target_pairs={{0,8},{8,0},{4,12},{12,4},{1,9},{9,1},{5,13},{13,5},{2,10},{10,2},... | collective-permute-start | bytes 3575816 | tf_op jit(solution)/shard_map/ppermute | solution.py:36
  196.6 28.0 %collective-permute-start.36 = (bf16[2,208,384]{2,1,0:T(8,128)(2,1)S(1)}, bf16[2,208,384]{2,1,0:T(8,128)(2,1)S(1)}, u32[]{:S(2)}, u32[]{:S(2)}) collective-permute-start(bf16[2,208,384]{2,1,0:T(8,128)(2,1)S(1)} %get-tuple-element.134), channel_id=1, source_target_pairs={{0,8},{8,0},{4,12},{12,4},{1,9},{9,1},{5,13},{13,5},{2,10},{10,2},... | collective-permute-start | bytes 958472 | tf_op jit(solution)/shard_map/ppermute | solution.py:36
  198.1 26.5 %collective-permute-start.37 = (bf16[2,208,384]{2,1,0:T(8,128)(2,1)S(1)}, bf16[2,208,384]{2,1,0:T(8,128)(2,1)S(1)}, u32[]{:S(2)}, u32[]{:S(2)}) collective-permute-start(bf16[2,208,384]{2,1,0:T(8,128)(2,1)S(1)} %get-tuple-element.136), channel_id=1, source_target_pairs={{0,4},{4,0},{8,12},{12,8},{1,5},{5,1},{9,13},{13,9},{2,6},{6,2},{1... | collective-permute-start | bytes 958472 | tf_op jit(solution)/shard_map/ppermute | solution.py:32
  224.8 15.6 %collective-permute-start.38 = (bf16[4,208,384]{2,1,0:T(8,128)(2,1)S(1)}, bf16[4,208,384]{2,1,0:T(8,128)(2,1)S(1)}, u32[]{:S(2)}, u32[]{:S(2)}) collective-permute-start(bf16[4,208,384]{2,1,0:T(8,128)(2,1)S(1)} %get-tuple-element.137), channel_id=1, source_target_pairs={{0,4},{4,0},{8,12},{12,8},{1,5},{5,1},{9,13},{13,9},{2,6},{6,2},{1... | collective-permute-start | bytes 1916936 | tf_op jit(solution)/shard_map/ppermute | solution.py:32
  228.5 19.9 %collective-permute-start.30 = (bf16[265,384]{1,0:T(8,128)(2,1)S(1)}, bf16[265,384]{1,0:T(8,128)(2,1)S(1)}, u32[]{:S(2)}, u32[]{:S(2)}) collective-permute-start(bf16[265,384]{1,0:T(8,128)(2,1)S(1)} %get-tuple-element.112), channel_id=1, source_target_pairs={{0,0},{1,1},{16,2},{17,3},{2,16},{3,17},{18,18},{19,19},{4,4},{5,5... | collective-permute-start | bytes 610568 | tf_op jit(solution)/shard_map/ppermute | solution.py:65
  240.9 30.4 %collective-permute-start.40 = (bf16[2,208,384]{2,1,0:T(8,128)(2,1)S(1)}, bf16[2,208,384]{2,1,0:T(8,128)(2,1)S(1)}, u32[]{:S(2)}, u32[]{:S(2)}) collective-permute-start(bf16[2,208,384]{2,1,0:T(8,128)(2,1)S(1)} %get-tuple-element.140), channel_id=1, source_target_pairs={{0,16},{16,0},{1,17},{17,1},{2,18},{18,2},{3,19},{19,3},{4,20},{20... | collective-permute-start | bytes 958472 | tf_op jit(solution)/shard_map/ppermute | solution.py:41
  242.0 31.6 %collective-permute-start.46 = (bf16[400,384]{1,0:T(8,128)(2,1)S(1)}, bf16[400,384]{1,0:T(8,128)(2,1)S(1)}, u32[]{:S(2)}, u32[]{:S(2)}) collective-permute-start(bf16[400,384]{1,0:T(8,128)(2,1)S(1)} %get-tuple-element.151), channel_id=1, source_target_pairs={{0,1},{1,2},{2,3},{3,0},{4,5},{5,6},{6,7},{7,4},{8,9},{9,10},{10,1... | collective-permute-start | bytes 921608 | tf_op jit(solution)/shard_map/ppermute | solution.py:46
  244.9 40.7 %collective-permute-start.47 = (bf16[400,384]{1,0:T(8,128)(2,1)S(1)}, bf16[400,384]{1,0:T(8,128)(2,1)S(1)}, u32[]{:S(2)}, u32[]{:S(2)}) collective-permute-start(bf16[400,384]{1,0:T(8,128)(2,1)S(1)} %get-tuple-element.152), channel_id=1, source_target_pairs={{0,2},{1,3},{2,0},{3,1},{4,6},{5,7},{6,4},{7,5},{8,10},{9,11},{10,... | collective-permute-start | bytes 921608 | tf_op jit(solution)/shard_map/ppermute | solution.py:46
  245.5 40.1 %collective-permute-start.48 = (bf16[400,384]{1,0:T(8,128)(2,1)S(1)}, bf16[400,384]{1,0:T(8,128)(2,1)S(1)}, u32[]{:S(2)}, u32[]{:S(2)}) collective-permute-start(bf16[400,384]{1,0:T(8,128)(2,1)S(1)} %get-tuple-element.153), channel_id=1, source_target_pairs={{0,3},{1,0},{2,1},{3,2},{4,7},{5,4},{6,5},{7,6},{8,11},{9,8},{10,9... | collective-permute-start | bytes 921608 | tf_op jit(solution)/shard_map/ppermute | solution.py:46
  248.3 22.4 %collective-permute-start.31 = (bf16[265,384]{1,0:T(8,128)(2,1)S(1)}, bf16[265,384]{1,0:T(8,128)(2,1)S(1)}, u32[]{:S(2)}, u32[]{:S(2)}) collective-permute-start(bf16[265,384]{1,0:T(8,128)(2,1)S(1)} %get-tuple-element.113), channel_id=1, source_target_pairs={{1,0},{0,1},{17,2},{16,3},{3,16},{2,17},{19,18},{18,19},{5,4},{4,5... | collective-permute-start | bytes 610568 | tf_op jit(solution)/shard_map/ppermute | solution.py:65
  270.7 19.7 %collective-permute-start.34 = (bf16[265,384]{1,0:T(8,128)(2,1)S(1)}, bf16[265,384]{1,0:T(8,128)(2,1)S(1)}, u32[]{:S(2)}, u32[]{:S(2)}) collective-permute-start(bf16[265,384]{1,0:T(8,128)(2,1)S(1)} %get-tuple-element.130), channel_id=1, source_target_pairs={{0,0},{1,1},{16,2},{17,3},{2,16},{3,17},{18,18},{19,19},{4,4},{5,5... | collective-permute-start | bytes 610568 | tf_op jit(solution)/shard_map/ppermute | solution.py:65
  271.4 19.0 %collective-permute-start.35 = (bf16[265,384]{1,0:T(8,128)(2,1)S(1)}, bf16[265,384]{1,0:T(8,128)(2,1)S(1)}, u32[]{:S(2)}, u32[]{:S(2)}) collective-permute-start(bf16[265,384]{1,0:T(8,128)(2,1)S(1)} %get-tuple-element.131), channel_id=1, source_target_pairs={{1,0},{0,1},{17,2},{16,3},{3,16},{2,17},{19,18},{18,19},{5,4},{4,5... | collective-permute-start | bytes 610568 | tf_op jit(solution)/shard_map/ppermute | solution.py:65
  273.7 18.4 %collective-permute-start.41 = (bf16[208,384]{1,0:T(8,128)(2,1)S(1)}, bf16[208,384]{1,0:T(8,128)(2,1)S(1)}, u32[]{:S(2)}, u32[]{:S(2)}) collective-permute-start(bf16[208,384]{1,0:T(8,128)(2,1)S(1)} %get-tuple-element.142), channel_id=1, source_target_pairs={{0,3},{1,0},{2,1},{3,2},{4,7},{5,4},{6,5},{7,6},{8,11},{9,8},{10,9... | collective-permute-start | bytes 479240 | tf_op jit(solution)/shard_map/ppermute | solution.py:46
  285.6 19.8 %collective-permute-start.42 = (bf16[208,384]{1,0:T(8,128)(2,1)S(1)}, bf16[208,384]{1,0:T(8,128)(2,1)S(1)}, u32[]{:S(2)}, u32[]{:S(2)}) collective-permute-start(bf16[208,384]{1,0:T(8,128)(2,1)S(1)} %get-tuple-element.143), channel_id=1, source_target_pairs={{0,2},{1,3},{2,0},{3,1},{4,6},{5,7},{6,4},{7,5},{8,10},{9,11},{10,... | collective-permute-start | bytes 479240 | tf_op jit(solution)/shard_map/ppermute | solution.py:46
  285.6 19.8 %collective-permute-start.43 = (bf16[208,384]{1,0:T(8,128)(2,1)S(1)}, bf16[208,384]{1,0:T(8,128)(2,1)S(1)}, u32[]{:S(2)}, u32[]{:S(2)}) collective-permute-start(bf16[208,384]{1,0:T(8,128)(2,1)S(1)} %get-tuple-element.144), channel_id=1, source_target_pairs={{0,1},{1,2},{2,3},{3,0},{4,5},{5,6},{6,7},{7,4},{8,9},{9,10},{10,1... | collective-permute-start | bytes 479240 | tf_op jit(solution)/shard_map/ppermute | solution.py:46
  (31 other events, 329.9 us)
